TPU v7x, 128 devices: a whole 4x4x4 slice. The times are simulated.
128 devices in a mesh: dp: 4 (over x), expert: 8 (over z, core), tensor: 4 (over y).
Axes of the slice: x: 4, y: 4, z: 4, core: 2. Of those that a mesh axis runs over, the one named last changes fastest.
Arguments:
- tokens: bfloat16 [4096, 2048], P(('dp', 'expert')), may hold values from -6 to 6
- cotangent: bfloat16 [4096, 2048], P(('dp', 'expert')), may hold values from -6 to 6
- seq_lengths: int32 [32, 3], P(('dp', 'expert')), may hold values from 1 to 64, 128 in all within a row
- deal_order: int32 [4096], P(('dp', 'expert')), may hold values from 0 to 4095, as said below
- expert_ids: int32 [4096, 8], P(('dp', 'expert')), may hold values from 0 to 15, all different within a row
- slot_order: int32 [4096, 8], P(('dp', 'expert')), may hold values from 0 to 1023, as said below
- qkv_weight: bfloat16 [3, 2048, 2048], P(None, ('dp', 'expert'), 'tensor'), may hold values from -0.125 to 0.125
- out_weight: bfloat16 [2048, 2048], P('tensor', ('dp', 'expert')), may hold values from -0.5 to 0.5
- router_weight: bfloat16 [16, 2048], P(None, ('dp', 'expert')), may hold values from -0.0625 to 0.0625
- gate_weight: bfloat16 [16, 2048, 1024], P('expert', 'dp', 'tensor'), may hold values from -0.125 to 0.125
- up_weight: bfloat16 [16, 2048, 1024], P('expert', 'dp', 'tensor'), may hold values from -0.125 to 0.125
- down_weight: bfloat16 [16, 2048, 1024], P('expert', 'dp', 'tensor'), may hold values from -0.75 to 0.75
- gain_first: float32 [2048], replicated, may hold values from 0.5 to 1.5
- gain_second: float32 [2048], replicated, may hold values from 0.5 to 1.5
Outputs:
- layer_out: bfloat16 [4096, 2048], P(('dp', 'expert'), 'tensor')
- input_grad: bfloat16 [4096, 2048], P(('dp', 'expert'), 'tensor')
- qkv_grad: float32 [3, 2048, 2048], P(None, ('dp', 'expert'), 'tensor')
- out_grad: float32 [2048, 2048], P('tensor', ('dp', 'expert'))
- router_grad: float32 [16, 2048], P(None, ('dp', 'expert'))
- gate_grad: float32 [16, 2048, 1024], P('expert', 'dp', 'tensor')
- up_grad: float32 [16, 2048, 1024], P('expert', 'dp', 'tensor')
- down_grad: float32 [16, 2048, 1024], P('expert', 'dp', 'tensor')
- gain_first_grad: float32 [2048], P(('dp', 'expert'))
- gain_second_grad: float32 [2048], P(('dp', 'expert'))
Inputs may be any that keep to these rules, and one draw needn't show every extreme that they name: `deal_order`: A permutation of the token rows. Row t of group g = t // 128 is dealt to a group d with d // 8 == g // 8, at a position from d * 128 + (g % 8) * 16 up to 16 more; each such block of 16 positions is filled from group g exactly. `slot_order`: in each aligned block of 128 rows the 1024 entries are a permutation. `seq_lengths`: each row sums to 128. `expert_ids`: each row names 8 different experts.
All inputs are finite; a program needn't handle non-finite values.
Results may differ from a plain program's by a relative error of at most 0.023.
Values may be sent and summed in bfloat16 or wider, within the bound.
No kernel may reach another device: no remote copies, remote signals or barrier semaphores. Data moves between devices by JAX's collectives and lax.ppermute only.
A program may use at most 128 MiB of HBM per device.

v0:
```python
import jax
import jax.numpy as jnp
from jax import lax
from jax.sharding import Mesh
from jax.sharding import PartitionSpec as P
from jax.experimental import pallas as pl
from jax.experimental.pallas import tpu as pltpu

HEAD_DIM = 128
EPSILON = 1e-05
F32 = jnp.float32
BF16 = jnp.bfloat16
BIG = 1 << 30
VMEM = pltpu.VMEM
ANY = pl.ANY


def shift(values, axis, step):
    size = lax.axis_size(axis)
    return lax.ppermute(values, axis, [(i, (i + step) % size) for i in range(size)])


def core_swap(values):
    return lax.ppermute(values, "core", [(0, 1), (1, 0)])


def gather_near(values, axis):
    size = lax.axis_size(axis)
    got = {k: shift(values, axis, -k) for k in (1, size - 1, 2)}
    return [values] + [got[k] for k in range(1, size)]


def gather_ring(values, axis):
    half = values.shape[0] // 2
    left, right = shift(values, axis, 1), shift(values, axis, -1)
    far = [shift(left[:half], axis, 1), shift(right[half:], axis, -1)]
    return [values, right, jnp.concatenate(far, axis=0), left]


def sum_near(parts, axis):
    size = lax.axis_size(axis)
    total = parts[0].astype(F32)
    for k in (1, size - 1, 2):
        total = total + shift(parts[k], axis, k).astype(F32)
    return total


def swap_near(parts, axis):
    size = lax.axis_size(axis)
    return [parts[0]] + [shift(parts[k], axis, k) for k in (1, size - 1, 2)]


def total(parts):
    return sum(part.astype(F32) for part in parts)


def segment_of(seq_lengths, row_count):
    seq_ends = jnp.cumsum(seq_lengths)
    position = jnp.arange(row_count, dtype=jnp.int32)
    return jnp.sum((position[:, None] >= seq_ends[None, :]).astype(jnp.int32), axis=1)


def nt(a,b): return lax.dot_general(a,b,(((1,),(1,)),((),())),preferred_element_type=F32)
def tn(a,b): return lax.dot_general(a,b,(((0,),(0,)),((),())),preferred_element_type=F32)

def spec(space):
    return pl.BlockSpec(memory_space=space)


def params(megabytes=62):
    return pltpu.CompilerParams(vmem_limit_bytes=megabytes * 1024 * 1024)


def cost(flops, moved):
    return pl.CostEstimate(flops=flops, bytes_accessed=moved, transcendentals=0)


def pack_kernel(qkv, out, router, packed):
    for s in range(3):
        packed[:, s * 512 : (s + 1) * 512] = qkv[s]
    packed[:, 1536:2048] = out[...]
    wide = jnp.concatenate([router[...].astype(F32), jnp.zeros((112, 64), F32)], axis=0)
    packed[:, 2048:] = wide.T.astype(BF16)


def pack_call(qkv, out, router):
    return pl.pallas_call(
        pack_kernel,
        out_shape=jax.ShapeDtypeStruct((64, 2176), BF16),
        cost_estimate=cost(1000, 6 * 10**5),
        compiler_params=params(),
        grid=(1,),
        name="pack",
    )(qkv, out, router)


def spread_features(values, out, row):
    count = values.shape[0]
    for e in range(8):
        for d in range(4):
            at = d * 512 + e * 64
            out[e, row : row + count, d * 64 : (d + 1) * 64] = values[:, at : at + 64]


def norm_kernel(tokens, gain, normed_out, feat_out):
    values = tokens[...].astype(F32)
    factor = lax.rsqrt(jnp.mean(values * values, axis=-1, keepdims=True) + EPSILON)
    normed = (values * factor * gain[...]).astype(BF16)
    normed_out[...] = normed
    spread_features(normed, feat_out, 0)


def norm_call(tokens, gain):
    shape = jax.ShapeDtypeStruct
    return pl.pallas_call(
        norm_kernel,
        out_shape=(shape((128, 2048), BF16), shape((8, 128, 256), BF16)),
        cost_estimate=cost(10**6, 15 * 10**5),
        compiler_params=params(),
        grid=(1,),
        name="norm",
    )(tokens, gain)


def attention_kernel(
    where, normed, same, packed, proj_out, prob_out, mixed_out, b0, b1, b2, b3, w_buf, o_buf, sem_w, sem_o
):
    y0 = where[0]
    loads = [
        pltpu.make_async_copy(packed.at[:, s * 512 : (s + 1) * 512], w_buf.at[s], sem_w.at[s])
        for s in range(3)
    ]
    for load in loads:
        load.start()
    out_load = pltpu.make_async_copy(packed.at[:, 1536:2048], o_buf, sem_o)
    out_load.start()
    for s in range(3):
        loads[s].wait()
        proj_out[s] = jnp.dot(normed[...], w_buf[s], preferred_element_type=F32).astype(BF16)
    mask = same[...] > 0.5
    scale = HEAD_DIM ** (-0.5)
    for h in range(4):
        cols = slice(h * HEAD_DIM, (h + 1) * HEAD_DIM)
        scores = jnp.where(
            mask, nt(proj_out[0, :, cols], proj_out[1, :, cols]) * scale, -1000000000.0
        )
        grown = jnp.exp(scores - jnp.max(scores, axis=-1, keepdims=True))
        prob = grown / jnp.sum(grown, axis=-1, keepdims=True)
        prob_out[h] = prob
        mixed_out[:, cols] = jnp.dot(
            prob.astype(BF16), proj_out[2, :, cols], preferred_element_type=F32
        ).astype(BF16)
    out_load.wait()
    for k, branch in enumerate((b0, b1, b2, b3)):
        at = pl.multiple_of(((y0 + k) & 3) * 512, 512)
        branch[...] = nt(mixed_out[...], o_buf[pl.ds(at, 512), :]).astype(BF16)


def attention_call(where, normed, same, packed):
    shape = jax.ShapeDtypeStruct
    dma = pltpu.SemaphoreType.DMA
    return pl.pallas_call(
        attention_kernel,
        out_shape=(
            shape((3, 128, 512), BF16),
            shape((4, 128, 128), F32),
            shape((128, 512), BF16),
        )
        + (shape((128, 512), BF16),) * 4,
        in_specs=[spec(pltpu.SMEM), spec(VMEM), spec(VMEM), spec(ANY)],
        out_specs=(spec(VMEM),) * 7,
        scratch_shapes=[VMEM((3, 2048, 512), BF16), VMEM((2048, 512), BF16), dma((3,)), dma],
        compiler_params=params(),
        cost_estimate=cost(2 * 10**9, 10 * 10**6),
        grid=(1,),
        name="attention",
    )(where, normed, same, packed)


def attention_back_kernel(
    where, g0, g1, g2, g3, dots, gates, hidden, resid, cots, packed, proj_in, prob_in, gain,
    feat_out, grad_proj, own_out,
    o_buf, h_buf, c_buf, x_buf, d_buf, x_low, d_low, proj, prob, sem_o, sem_h, sem_c, sem_x, sem_d, sem_p,
):
    y0 = where[0]
    offs = [pl.multiple_of(((y0 + k) & 3) * 512, 512) for k in range(4)]
    d_loads = [
        pltpu.make_async_copy(g, d_low.at[:, pl.ds(offs[k], 512)], sem_d.at[k])
        for k, g in enumerate((g0, g1, g2, g3))
    ]
    x_loads = [
        pltpu.make_async_copy(resid.at[k], x_low.at[:, pl.ds(offs[k], 512)], sem_x.at[k])
        for k in range(4)
    ]
    h_load = pltpu.make_async_copy(hidden.at[0:128], h_buf, sem_h)
    o_load = pltpu.make_async_copy(packed.at[:, 1536:2176], o_buf, sem_o)
    c_load = pltpu.make_async_copy(cots, c_buf, sem_c)
    p_loads = [
        pltpu.make_async_copy(proj_in, proj, sem_p.at[0]),
        pltpu.make_async_copy(prob_in, prob, sem_p.at[1]),
    ]
    for load in [*x_loads, *d_loads, h_load, o_load, c_load, *p_loads]:
        load.start()
    for load in [*x_loads, *d_loads]:
        load.wait()
    x_buf[...] = x_low[...].astype(F32)
    d_buf[...] = d_low[...].astype(F32)
    share = gates[...]
    dot = dots[...]
    grad_logits = (share * (dot - jnp.sum(dot * share, axis=-1, keepdims=True))).astype(BF16)
    o_load.wait()
    h_load.wait()
    router = tn(grad_logits, h_buf[...])
    grad_hidden = d_buf[...] + nt(grad_logits, o_buf[:, 512:])
    resid_rows = x_buf[...]
    factor = lax.rsqrt(jnp.mean(resid_rows * resid_rows, axis=-1, keepdims=True) + EPSILON)
    unit = resid_rows * factor
    gain_sum = jnp.sum(grad_hidden * unit, axis=0, keepdims=True)
    scaled = grad_hidden * gain[...]
    c_load.wait()
    grad = c_buf[...].astype(F32) + factor * (
        scaled - unit * jnp.mean(scaled * unit, axis=-1, keepdims=True)
    )
    d_buf[...] = grad
    own_out[...] = d_buf[:, pl.ds(offs[0], 512)]
    low = grad.astype(BF16)
    spread_features(low, feat_out, 0)
    spread_features(router[:16].astype(BF16), feat_out, 128)
    high = gain_sum.astype(BF16)
    rest = (gain_sum - high.astype(F32)).astype(BF16)
    tail = jnp.concatenate(
        [high.astype(F32), rest.astype(F32), jnp.zeros((14, 2048), F32)], axis=0
    ).astype(BF16)
    spread_features(tail, feat_out, 144)
    mixed = jnp.dot(low, o_buf[:, :512], preferred_element_type=F32).astype(BF16)
    for load in p_loads:
        load.wait()
    scale = HEAD_DIM ** (-0.5)
    for h in range(4):
        cols = slice(h * HEAD_DIM, (h + 1) * HEAD_DIM)
        weights = prob[h]
        back = mixed[:, cols]
        grad_proj[:, 1024 + h * HEAD_DIM : 1024 + (h + 1) * HEAD_DIM] = tn(
            weights.astype(BF16), back
        ).astype(BF16)
        weight_grad = nt(back, proj[2, :, cols])
        offset = jnp.sum(weight_grad * weights, axis=-1, keepdims=True)
        score = (weights * (weight_grad - offset)).astype(BF16)
        grad_proj[:, cols] = (
            jnp.dot(score, proj[1, :, cols], preferred_element_type=F32) * scale
        ).astype(BF16)
        grad_proj[:, 512 + h * HEAD_DIM : 512 + (h + 1) * HEAD_DIM] = (
            tn(score, proj[0, :, cols]) * scale
        ).astype(BF16)


def attention_back_call(where, grads, dots, gates, hidden, resid, cots, packed, proj, prob, gain):
    shape = jax.ShapeDtypeStruct
    dma = pltpu.SemaphoreType.DMA
    return pl.pallas_call(
        attention_back_kernel,
        out_shape=(
            shape((8, 160, 256), BF16),
            shape((128, 1536), BF16),
            shape((128, 512), F32),
        ),
        in_specs=[spec(pltpu.SMEM)]
        + [spec(ANY)] * 4
        + [spec(VMEM)] * 2
        + [spec(ANY)] * 6
        + [spec(VMEM)],
        out_specs=(spec(VMEM),) * 3,
        scratch_shapes=[
            VMEM((2048, 640), BF16),
            VMEM((128, 2048), BF16),
            VMEM((128, 2048), BF16),
            VMEM((128, 2048), F32),
            VMEM((128, 2048), F32),
            VMEM((128, 2048), BF16),
            VMEM((128, 2048), BF16),
            VMEM((3, 128, 512), BF16),
            VMEM((4, 128, 128), F32),
            dma,
            dma,
            dma,
            dma((4,)),
            dma((4,)),
            dma((2,)),
        ],
        compiler_params=params(),
        cost_estimate=cost(10**9, 6 * 10**6),
        grid=(1,),
        name="attention_back",
    )(where, *grads, dots, gates, hidden, resid, cots, packed, proj, prob, gain)


def normed_back_kernel(where, grad_proj, tokens, gain, packed, o0, o1, o2, o3, w_buf, sem_w):
    y0 = where[0]
    outs = (o0, o1, o2, o3)
    order = [(y0 + k) & 3 for k in (1, 3, 2, 0)]
    loads = [
        pltpu.make_async_copy(
            packed.at[pl.ds(pl.multiple_of(at * 512, 512), 512), 0:1536], w_buf.at[i], sem_w.at[i]
        )
        for i, at in enumerate(order)
    ]
    for load in loads:
        load.start()
    values = tokens[...].astype(F32)
    factor = lax.rsqrt(jnp.mean(values * values, axis=-1, keepdims=True) + EPSILON)
    inner = jnp.zeros((128, 1), F32)
    sums = []
    for i, k in enumerate((1, 3, 2, 0)):
        loads[i].wait()
        grad = nt(grad_proj[...], w_buf[i])
        cols = pl.ds(pl.multiple_of(order[i] * 512, 512), 512)
        unit = tokens[:, cols].astype(F32) * factor
        inner = inner + jnp.sum(grad * unit * gain[:, cols], axis=-1, keepdims=True)
        sums.append(jnp.sum(grad * unit, axis=0, keepdims=True))
        outs[k][0:128, 0:512] = grad.astype(BF16)
    lane = lax.broadcasted_iota(jnp.int32, (128, 128), 1)
    high = inner.astype(BF16).astype(F32)
    both = jnp.where(lane == 0, high, jnp.where(lane == 1, inner - high, 0.0)).astype(BF16)
    row = lax.broadcasted_iota(jnp.int32, (16, 512), 0)
    table = jnp.zeros((16, 512), F32)
    for at, piece in zip(order, sums):
        top = piece.astype(BF16).astype(F32)
        table = jnp.where(row == at, top, jnp.where(row == at + 4, piece - top, table))
    for out in outs:
        out[0:128, 512:] = both
        out[128:, 0:512] = table.astype(BF16)
        out[128:, 512:] = jnp.zeros((16, 128), BF16)


def normed_back_call(where, grad_proj, tokens, gain, packed):
    return pl.pallas_call(
        normed_back_kernel,
        out_shape=(jax.ShapeDtypeStruct((144, 640), BF16),) * 4,
        in_specs=[spec(pltpu.SMEM), spec(VMEM), spec(VMEM), spec(VMEM), spec(ANY)],
        out_specs=(spec(VMEM),) * 4,
        scratch_shapes=[VMEM((4, 512, 1536), BF16), pltpu.SemaphoreType.DMA((4,))],
        compiler_params=params(),
        cost_estimate=cost(10**9, 8 * 10**6),
        grid=(1,),
        name="normed_back",
    )(where, grad_proj, tokens, gain, packed)


def pair_kernel(own, other, *outs):
    for k, out in enumerate(outs):
        out[...] = own[k] + other[k]


def pair_call(own, other):
    shape = own.shape[1:]
    block = (shape[0] // 4,) + shape[1:]
    rest = (0,) * (len(shape) - 1)
    return pl.pallas_call(
        pair_kernel,
        out_shape=(jax.ShapeDtypeStruct(shape, BF16),) * 4,
        grid=(4,),
        in_specs=[pl.BlockSpec((4,) + block, lambda i: (0, i) + rest)] * 2,
        out_specs=(pl.BlockSpec(block, lambda i: (i,) + rest),) * 4,
        compiler_params=params(),
        cost_estimate=cost(10**6, 6 * own.size),
        name="pair",
    )(own, other)


def join_dots(table):
    return jnp.concatenate(
        [table[0:16], table[16:32], jnp.zeros((16, 256), F32)], axis=1
    ).astype(BF16)


def combine_kernel(p0, p1, p2, p3, *outs):
    for r, out in enumerate(outs):
        total = (p0[r].astype(F32) + p1[r].astype(F32)) + (p2[r].astype(F32) + p3[r].astype(F32))
        out[0:128] = total[0:128].astype(BF16)
        dots = total[128:, 0:128] + total[128:, 128:256]
        high = dots.astype(BF16).astype(F32)
        out[128:] = join_dots(jnp.concatenate([high, dots - high], axis=0))


def combine_call(pieces):
    return pl.pallas_call(
        combine_kernel,
        out_shape=(jax.ShapeDtypeStruct((144, 512), BF16),) * 4,
        grid=(1,),
        compiler_params=params(),
        cost_estimate=cost(10**6, 3 * 10**6),
        name="combine",
    )(*pieces)


def finish_kernel(p0, p1, p2, p3, cols, dots):
    total = (p0[...].astype(F32) + p1[...].astype(F32)) + (p2[...].astype(F32) + p3[...].astype(F32))
    cols[...] = total[0:128].astype(BF16)
    table = total[128:, 0:128] + total[128:, 128:256]
    dots[...] = jnp.concatenate([table, jnp.zeros((112, 128), F32)], axis=0).T


def finish_call(pieces):
    shape = jax.ShapeDtypeStruct
    return pl.pallas_call(
        finish_kernel,
        out_shape=(shape((128, 512), BF16), shape((128, 128), F32)),
        cost_estimate=cost(10**6, 10**6),
        compiler_params=params(),
        grid=(1,),
        name="finish",
    )(*pieces)


def columns_kernel(where, p0, p1, p2, p3, *outs):
    y0 = where[0]
    for k, out in enumerate(outs):
        cols = pl.ds(pl.multiple_of(((y0 + k) & 3) * 512, 512), 512)
        total = (p0[:, cols].astype(F32) + p1[:, cols].astype(F32)) + (
            p2[:, cols].astype(F32) + p3[:, cols].astype(F32)
        )
        out[...] = total.astype(BF16)


def columns_call(where, pieces):
    return pl.pallas_call(
        columns_kernel,
        out_shape=(jax.ShapeDtypeStruct((128, 512), BF16),) * 4,
        grid=(4,),
        in_specs=[spec(pltpu.SMEM)] + [pl.BlockSpec((32, 2048), lambda i: (i, 0))] * 4,
        out_specs=(pl.BlockSpec((32, 512), lambda i: (i, 0)),) * 4,
        compiler_params=params(),
        cost_estimate=cost(10**6, 3 * 10**6),
        name="columns",
    )(where, *pieces)


def tail_kernel(
    where, normed, own, other, branch, mixed, o0, o1, o2, o3, n_buf, p_buf, a_buf, sem
):
    me, d0 = where[1], where[2]
    loads = [
        pltpu.make_async_copy(piece.at[r], p_buf.at[pl.ds((c * 4 + r) * 128, 128)], sem.at[c, r])
        for c, piece in enumerate((own, other))
        for r in range(4)
    ]
    for load in loads:
        load.start()
    for r in range(8):
        at = (((me >> 1) + (r & 3)) & 3) * 2 + (((me & 1) + (r >> 2)) & 1)
        n_buf[r * 128 : (r + 1) * 128] = normed[at]
    a_buf[:, 1536:2048] = tn(branch[:, 0:128, :].reshape(1024, 256), mixed[...])
    small = jnp.sum(branch[:, 128:160, :].astype(F32), axis=0)
    a_buf[:, 2048:] = jnp.concatenate([small, jnp.zeros((96, 256), F32)], axis=0).T
    for load in loads:
        load.wait()
    for s in range(3):
        a_buf[:, s * 512 : (s + 1) * 512] = tn(n_buf[...], p_buf[:, s * 512 : (s + 1) * 512])
    for k, out in enumerate((o0, o1, o2, o3)):
        out[...] = a_buf[pl.ds(pl.multiple_of(((d0 + k) & 3) * 64, 64), 64), :].astype(BF16)


def tail_call(where, normed, own, other, branch, mixed):
    dma = pltpu.SemaphoreType.DMA
    return pl.pallas_call(
        tail_kernel,
        out_shape=(jax.ShapeDtypeStruct((64, 2176), BF16),) * 4,
        in_specs=[spec(pltpu.SMEM), spec(VMEM), spec(ANY), spec(ANY)] + [spec(VMEM)] * 2,
        out_specs=(spec(VMEM),) * 4,
        scratch_shapes=[
            VMEM((1024, 256), BF16),
            VMEM((1024, 1536), BF16),
            VMEM((256, 2176), F32),
            dma((2, 4)),
        ],
        compiler_params=params(),
        cost_estimate=cost(10**9, 8 * 10**6),
        grid=(1,),
        name="tail",
    )(where, normed, own, other, branch, mixed)


def block_row(me, r, s):
    group = (((me >> 1) + (r & 3)) & 3) * 2 + (((me & 1) + (r >> 2)) & 1)
    source = (((s >> 1) - (me >> 1)) & 3) + (((s & 1) + (me & 1)) & 1) * 4
    return pl.multiple_of(r * 128 + s * 16, 16), pl.multiple_of(source * 128 + group * 16, 16)


def back_kernel(
    where, g_own, g_other, w0, w1, w2, w3, g_out, back, own_rows, w_out,
    g_buf, w_buf, z_buf, sem_g, sem_w, sem_o,
):
    y0, me = where[0], where[1]
    offs = [pl.multiple_of(((y0 + k) & 3) * 512, 512) for k in range(4)]
    loads = [
        pltpu.make_async_copy(
            piece.at[k], g_buf.at[pl.ds(c * 512, 512), pl.ds(offs[k], 512)], sem_g.at[c, k]
        )
        for c, piece in enumerate((g_own, g_other))
        for k in range(4)
    ]
    w_loads = [
        pltpu.make_async_copy(
            piece,
            w_buf.at[:, pl.ds(pl.multiple_of(((where[2] + k) & 3) * 512, 512), 512), :],
            sem_w.at[k],
        )
        for k, piece in enumerate((w0, w1, w2, w3))
    ]
    for load in loads + w_loads:
        load.start()
    for load in loads:
        load.wait()
    out = pltpu.make_async_copy(g_buf, g_out, sem_o.at[0])
    out.start()
    for load in w_loads:
        load.wait()
    down_out = pltpu.make_async_copy(w_buf, w_out, sem_o.at[1])
    down_out.start()
    for e in range(2):
        z_buf[:, e * 256 : (e + 1) * 256] = jnp.dot(g_buf[...], w_buf[e], preferred_element_type=F32)

    def move(i, _):
        to, at = block_row(me, i >> 3, i & 7)
        back[pl.ds(to, 16), :] = z_buf[pl.ds(at, 16), :]
        return 0

    lax.fori_loop(0, 64, move, 0)
    for s in range(8):
        _, at = block_row(me, 0, s)
        own_rows[s * 16 : (s + 1) * 16, :] = g_buf[pl.ds(at, 16), :]
    out.wait()
    down_out.wait()


def back_call(where, g_own, g_other, down):
    shape = jax.ShapeDtypeStruct
    dma = pltpu.SemaphoreType.DMA
    return pl.pallas_call(
        back_kernel,
        out_shape=(shape((1024, 2048), BF16), shape((1024, 512), F32), shape((128, 2048), BF16), shape((2, 2048, 256), BF16)),
        in_specs=[spec(pltpu.SMEM)] + [spec(ANY)] * 6,
        out_specs=(spec(ANY), spec(VMEM), spec(VMEM), spec(ANY)),
        scratch_shapes=[
            VMEM((1024, 2048), BF16),
            VMEM((2, 2048, 256), BF16),
            VMEM((1024, 512), F32),
            dma((2, 4)),
            dma((4,)),
            dma((2,)),
        ],
        compiler_params=params(),
        cost_estimate=cost(2 * 10**9, 13 * 10**6),
        grid=(1,),
        name="back",
    )(where, g_own, g_other, *down)


def expert_kernel(
    where, near_own, far_own, near_other, far_other, back, code, weights, packed, gain,
    sent_own, sent_other, h_out, mid_out, source_out, gates_out,
    x_buf, b_buf, w_buf, h_buf, d_buf, r_buf, mid, by_source,
    sem_x, sem_b, sem_w, sem_r, sem_h, sem_m, sem_d,
):
    y0, me = where[0], where[1]
    offs = [pl.multiple_of(((y0 + k) & 3) * 512, 512) for k in range(4)]
    x_loads = [
        [
            pltpu.make_async_copy(piece, x_buf.at[b, r], sem_x.at[b, r])
            for r, piece in enumerate((near.at[0], near.at[1], far, near.at[2]))
        ]
        for b, (near, far) in enumerate(((near_own, far_own), (near_other, far_other)))
    ]
    w_load = pltpu.make_async_copy(weights.at[pl.ds(0, 4)], w_buf, sem_w)
    r_load = pltpu.make_async_copy(packed.at[:, 2048:2176], r_buf, sem_r)
    b_load = pltpu.make_async_copy(back, b_buf, sem_b)
    for load in x_loads[0]:
        load.start()
    r_load.start()
    w_load.start()
    b_load.start()
    for load in x_loads[1]:
        load.start()
    stores = []
    lane = lax.broadcasted_iota(jnp.int32, (512, 128), 1)
    for b in range(2):
        for load in x_loads[b]:
            load.wait()

        def norm(r, _):
            square = jnp.zeros((128, 1), F32)
            for k in range(4):
                value = x_buf[b, r, k].astype(F32)
                square = square + jnp.sum(value * value, axis=-1, keepdims=True)
            factor = lax.rsqrt(square * (1.0 / 2048) + EPSILON)
            at = pl.ds(pl.multiple_of(b * 512 + r * 128, 128), 128)
            for k in range(4):
                part = gain[pl.ds((y0 + k) & 3, 1), :]
                h_buf[at, pl.ds(offs[k], 512)] = (x_buf[b, r, k].astype(F32) * factor * part).astype(BF16)
            return 0

        lax.fori_loop(0, 4, norm, 0)
        here = pl.ds(b * 512, 512)
        stores.append(pltpu.make_async_copy(h_buf.at[here], h_out.at[here], sem_h.at[b]))
        stores[-1].start()
        if b == 0:
            r_load.wait()
        logits = jnp.dot(h_buf[here, :], r_buf[...], preferred_element_type=F32)
        codes = code[here, :].astype(F32)
        chosen = codes > 0.5
        top = jnp.max(jnp.where(chosen, logits, -jnp.inf), axis=-1, keepdims=True)
        lifted = jnp.where(chosen, jnp.exp(logits - top), 0.0)
        gates = lifted / jnp.sum(lifted, axis=-1, keepdims=True)
        if b == 0:
            gates_out[...] = gates[:128]
            w_load.wait()
            b_load.wait()
        used = jnp.where(codes > 1.5, gates, 0.0)
        dots = jnp.zeros((512, 128), F32)
        for e in range(2):
            mine = lane == me * 2 + e
            use = jnp.sum(jnp.where(mine, used, 0.0), axis=-1, keepdims=True)
            keep = jnp.sum(jnp.where(mine & (codes > 1.5), 1.0, 0.0), axis=-1, keepdims=True)
            cols = pl.ds(e * 256, 256)
            u = jnp.dot(h_buf[here, :], w_buf[e], preferred_element_type=F32)
            w = jnp.dot(h_buf[here, :], w_buf[2 + e], preferred_element_type=F32)
            z = b_buf[here, cols]
            s = 1.0 / (1.0 + jnp.exp(-u))
            silu = u * s
            act = silu * w
            dot = jnp.sum(z * act, axis=-1, keepdims=True) * keep
            high = dot.astype(BF16).astype(F32)
            dots = jnp.where(mine, high, dots)
            dots = jnp.where(lane == me * 2 + e + 16, dot - high, dots)
            z = z * use
            mid[0, here, cols] = (z * w * s * (1.0 + u * (1.0 - s))).astype(BF16)
            mid[1, here, cols] = (z * silu).astype(BF16)
            mid[2, here, cols] = (act * use).astype(BF16)
        turned = [join_dots(dots[r * 128 : (r + 1) * 128].T) for r in range(4)]
        for k in range(4):
            acc = None
            for e in range(2):
                for m in range(2):
                    term = nt(mid[m, here, pl.ds(e * 256, 256)], w_buf[2 * m + e, pl.ds(offs[k], 512), :])
                    acc = term if acc is None else acc + term
            acc = acc.astype(BF16)
            for r in range(4):
                d_buf[b, k, r, 0:128] = acc[r * 128 : (r + 1) * 128]
                d_buf[b, k, r, 128:] = turned[r]
            target = (sent_own, sent_other)[b].at[k]
            stores.append(pltpu.make_async_copy(d_buf.at[b, k], target, sem_d.at[b, k]))
            stores[-1].start()
    stores.append(pltpu.make_async_copy(mid, mid_out, sem_m.at[0]))
    stores[-1].start()

    def move(i, _):
        at, to = block_row(me, i >> 3, i & 7)
        by_source[pl.ds(to, 16), :] = mid[2, pl.ds(at, 16), :]
        return 0

    lax.fori_loop(0, 64, move, 0)
    stores.append(pltpu.make_async_copy(by_source, source_out, sem_m.at[1]))
    stores[-1].start()
    for store in stores:
        store.wait()


def experts_call(where, resid, back, code, weights, packed, gain):
    shape = jax.ShapeDtypeStruct
    dma = pltpu.SemaphoreType.DMA
    return pl.pallas_call(
        expert_kernel,
        out_shape=(
            shape((4, 4, 144, 512), BF16),
            shape((4, 4, 144, 512), BF16),
            shape((1024, 2048), BF16),
            shape((3, 1024, 512), BF16),
            shape((1024, 512), BF16),
            shape((128, 128), F32),
        ),
        in_specs=[spec(pltpu.SMEM)]
        + [spec(ANY)] * 5
        + [spec(VMEM)]
        + [spec(ANY)] * 2
        + [spec(VMEM)],
        out_specs=(spec(ANY),) * 5 + (spec(VMEM),),
        scratch_shapes=[
            VMEM((2, 4, 4, 128, 512), BF16),
            VMEM((1024, 512), F32),
            VMEM((4, 2048, 256), BF16),
            VMEM((1024, 2048), BF16),
            VMEM((2, 4, 4, 144, 512), BF16),
            VMEM((2048, 128), BF16),
            VMEM((3, 1024, 512), BF16),
            VMEM((1024, 512), BF16),
            dma((2, 4)),
            dma,
            dma,
            dma,
            dma((2,)),
            dma((2,)),
            dma((2, 4)),
        ],
        compiler_params=params(),
        cost_estimate=cost(9 * 10**9, 26 * 10**6),
        grid=(1,),
        name="experts",
    )(where, *resid, back, code, weights, packed, gain)


def grads_kernel(h, g, mid, by_source, out):
    for i, (rows, cols) in enumerate(((h, mid[0]), (h, mid[1]), (g, by_source[...]))):
        grad = tn(rows[...], cols)
        for e in range(2):
            out[0, 2 * i + e] = grad[:, e * 256 : (e + 1) * 256].astype(BF16)


def grads_call(h, g, mid, by_source):
    return pl.pallas_call(
        grads_kernel,
        grid=(4,),
        out_shape=jax.ShapeDtypeStruct((4, 6, 512, 256), BF16),
        in_specs=[
            pl.BlockSpec((1024, 512), lambda j: (0, j)),
            pl.BlockSpec((1024, 512), lambda j: (0, j)),
            pl.BlockSpec((2, 1024, 512), lambda j: (0, 0, 0)),
            pl.BlockSpec((1024, 512), lambda j: (0, 0)),
        ],
        out_specs=pl.BlockSpec((1, 6, 512, 256), lambda j: (j, 0, 0, 0)),
        compiler_params=params(),
        cost_estimate=cost(7 * 10**9, 18 * 10**6),
        name="grads",
    )(h, g, mid, by_source)


def rows_kernel(mid, w, own, other):
    acc = nt(mid[0, :, 0:256], w[0]) + nt(mid[0, :, 256:512], w[1])
    own[...] = acc[:512].astype(BF16)
    other[...] = acc[512:].astype(BF16)


def rows_call(mid, weights):
    shape = jax.ShapeDtypeStruct
    return pl.pallas_call(
        rows_kernel,
        grid=(4,),
        out_shape=(shape((512, 2048), BF16),) * 2,
        in_specs=[
            pl.BlockSpec((1, 1024, 512), lambda j: (2, 0, 0)),
            pl.BlockSpec((2, 512, 256), lambda j: (0, j, 0)),
        ],
        out_specs=(pl.BlockSpec((512, 512), lambda j: (0, j)),) * 2,
        compiler_params=params(),
        cost_estimate=cost(2 * 10**9, 7 * 10**6),
        name="rows",
    )(mid, weights)


def local(
    tokens,
    cotangent,
    seq_lengths,
    deal_order,
    expert_ids,
    slot_order,
    qkv_weight,
    out_weight,
    router_weight,
    gate_weight,
    up_weight,
    down_weight,
    gain_first,
    gain_second,
):
    rows, width = tokens.shape
    zc = ("z", "core")
    peers = lax.axis_size("z") * lax.axis_size("core")
    tensors = lax.axis_size("tensor")
    dps = lax.axis_size("dp")
    zs = lax.axis_size("z")
    share = rows // peers
    part = width // tensors
    me_core = lax.axis_index("core")
    me_z = lax.axis_index("z")
    me = me_z * 2 + me_core
    me_y = lax.axis_index("tensor")
    experts = router_weight.shape[0]
    top = expert_ids.shape[1]
    capacity = (5 * rows * top + 4 * experts - 1) // (4 * experts)
    here = gate_weight.shape[0]
    head_width = qkv_weight.shape[2]
    feats = qkv_weight.shape[1]

    place_now = jnp.stack([me_y, me, lax.axis_index("dp")]).astype(jnp.int32)

    packed = lax.all_gather(
        pack_call(qkv_weight, out_weight.T, router_weight), ("dp", "z", "core"), axis=0, tiled=True
    )
    expert_local = jnp.concatenate([gate_weight, up_weight], axis=0)
    down_near = gather_ring(down_weight, "dp")

    dest_group = deal_order // rows % peers
    place = dest_group * share + (deal_order % rows - me * share)
    deal_matrix = (place[None, :] == jnp.arange(rows, dtype=jnp.int32)[:, None]).astype(BF16)
    dealt = jnp.dot(deal_matrix, tokens, preferred_element_type=F32).astype(BF16)
    cot_part = lax.dynamic_slice_in_dim(cotangent, me_y * part, part, 1)
    cot_part = jnp.dot(deal_matrix, cot_part, preferred_element_type=F32).astype(BF16)

    match = expert_ids[:, :, None] == jnp.arange(experts, dtype=jnp.int32)[None, None, :]
    order = jnp.min(jnp.where(match, slot_order[:, :, None], BIG), axis=1)
    chosen = order < BIG
    earlier = jnp.sum((order[None, :, :] < order[:, None, :]).astype(jnp.int32), axis=1)
    code = chosen.astype(F32) + (chosen & (earlier < capacity)).astype(F32)
    table = jnp.pad(code, ((0, 0), (0, 128 - experts))).astype(BF16)
    cot_near = gather_near(jnp.concatenate([cot_part, table], axis=1), "z")
    code_own = jnp.stack([near[:, part:] for near in cot_near])
    code_all = jnp.stack([code_own, core_swap(code_own)]).reshape(peers * rows, 128)
    cot_own = jnp.stack([near[:, :part] for near in cot_near])
    dealt, cot_own = lax.optimization_barrier((dealt, cot_own))
    got = lax.all_to_all(
        dealt.reshape(peers, share, width), zc, split_axis=0, concat_axis=0, tiled=True
    ).reshape(rows, width)
    cot_own = jnp.stack(gather_near(cot_own, "tensor")).reshape(tensors, zs * rows, part)

    segment = segment_of(seq_lengths[0], rows)
    same_seq = (segment[:, None] == segment[None, :]).astype(F32)
    normed, normed_feat = norm_call(got, gain_first.reshape(1, width))
    normed_feat = lax.all_to_all(normed_feat, zc, split_axis=0, concat_axis=0, tiled=True)
    expert_local, normed = lax.optimization_barrier((expert_local, normed))
    expert_full = lax.all_gather(expert_local, "dp", axis=1, tiled=True)
    normed, normed_feat, cot_own, code_all, packed, down_near = lax.optimization_barrier(
        (normed, normed_feat, cot_own, code_all, packed, down_near)
    )
    cot_other = core_swap(cot_own)
    projected, weights, mixed, *branch = attention_call(place_now, normed, same_seq, packed)
    mixed_all = lax.all_gather(mixed, zc, axis=0, tiled=True)
    resid_in = got.astype(F32)
    resid_part = lax.dynamic_slice_in_dim(resid_in, me_y * part, part, 1) + sum_near(
        branch, "tensor"
    )
    resid_near = jnp.stack(gather_near(resid_part.astype(BF16), "tensor"))
    resid_near, cot_other = lax.optimization_barrier((resid_near, cot_other))
    left, right = shift(resid_near, "z", 1), shift(resid_near, "z", -1)
    cot_all, back, upstream, down_full = back_call(place_now, cot_own, cot_other, down_near)
    half = tensors // 2
    left, right, back = lax.optimization_barrier((left, right, back))
    far = [shift(left[:half], "z", 1), shift(right[half:], "z", -1)]
    near_own = jnp.stack([resid_near, right, left])
    near_other = core_swap(near_own)
    far, near_other = lax.optimization_barrier((far, near_other))
    far_own = jnp.concatenate(far, axis=0)
    far_other = core_swap(far_own)

    sent_own, sent_other, hidden, mids, mid_source, gates = experts_call(
        place_now,
        (near_own, far_own, near_other, far_other),
        back,
        code_all,
        expert_full,
        packed,
        gain_second.reshape(tensors, part),
    )
    rows_own, rows_other = rows_call(mids, down_full)
    paired = pair_call(sent_own, core_swap(sent_other))
    paired, rows_own, rows_other = lax.optimization_barrier((paired, rows_own, rows_other))
    expert_rows = pair_call(
        rows_own.reshape(zs, rows, width), core_swap(rows_other).reshape(zs, rows, width)
    )
    expert_grads = grads_call(hidden, cot_all, mids, mid_source)
    cols, expert_rows, expert_grads = lax.optimization_barrier(
        (swap_near(paired, "tensor"), swap_near(expert_rows, "z"), expert_grads)
    )
    cols, expert_rows = lax.optimization_barrier((combine_call(cols), expert_rows))
    cols, expert_rows = lax.optimization_barrier(
        (swap_near(cols, "z"), columns_call(place_now, expert_rows))
    )
    cols, dots = finish_call(cols)
    grads_near, expert_rows = lax.optimization_barrier(
        (gather_near(cols, "tensor"), swap_near(expert_rows, "tensor"))
    )

    branch_feat, grad_proj, grad_own = attention_back_call(
        place_now,
        grads_near,
        dots,
        gates,
        hidden,
        resid_near,
        upstream,
        packed,
        projected,
        weights,
        gain_second.reshape(1, width),
    )
    grad_z = jnp.stack(gather_near(grad_proj, "z"))
    grad_other = core_swap(grad_z)
    branch_feat = lax.all_to_all(branch_feat, zc, split_axis=0, concat_axis=0, tiled=True)
    normed_cols = sum_near(
        normed_back_call(place_now, grad_proj, got, gain_first.reshape(1, width), packed), "tensor"
    )
    inner = normed_cols[:rows, part : part + 1] + normed_cols[:rows, part + 1 : part + 2]
    inner = inner / width
    gain_sum = (normed_cols[rows : rows + 4, :part] + normed_cols[rows + 4 : rows + 8, :part]).reshape(
        dps, peers, feats
    )
    gain_sum = gain_sum.transpose(1, 0, 2).reshape(peers, 1, dps * feats)
    gain_high = gain_sum.astype(BF16)
    gain_low = (gain_sum - gain_high.astype(F32)).astype(BF16)
    gain_rows = jnp.pad(
        jnp.concatenate([gain_high, gain_low], axis=1), ((0, 0), (0, 14), (0, 2 * part - dps * feats))
    )

    def own_cols(table):
        return lax.dynamic_slice_in_dim(table, me_y * part, part, table.ndim - 1)

    factor_first = lax.rsqrt(jnp.mean(resid_in * resid_in, axis=-1, keepdims=True) + EPSILON)
    input_part = grad_own + factor_first * (
        normed_cols[:rows, :part] * own_cols(gain_first) - own_cols(resid_in) * factor_first * inner
    )

    expert_grads = lax.psum_scatter(expert_grads, "dp", scatter_dimension=0, tiled=False)
    expert_grads = [expert_grads[here * i : here * (i + 1)].astype(F32) for i in range(3)]

    output_part = resid_part + total(expert_rows)

    final = jnp.concatenate([output_part.astype(BF16), input_part.astype(BF16)], axis=1)
    final = jnp.concatenate([final.reshape(peers, share, 2 * part), gain_rows], axis=1)
    final = lax.all_to_all(final, zc, split_axis=0, concat_axis=0, tiled=True)
    by_dp = tail_call(place_now, normed_feat, grad_z, grad_other, branch_feat, mixed_all)
    final, _ = lax.optimization_barrier((final, by_dp))
    gain_sum = jnp.sum(final[:, share : share + 2, : dps * feats].astype(F32), axis=(0, 1))
    gain_sum = gain_sum.reshape(dps, 1, feats)
    dp_index = lax.axis_index("dp")
    gain_sum = [
        lax.dynamic_index_in_dim(gain_sum, (dp_index + k) % dps, 0, keepdims=False) for k in range(dps)
    ]
    final = lax.dot_general(
        deal_matrix,
        final[:, :share].reshape(rows, 2 * part),
        (((0,), (0,)), ((), ())),
        preferred_element_type=F32,
    ).astype(BF16)
    by_dp, gain_sum, final, expert_grads = lax.optimization_barrier(
        (swap_near(by_dp, "dp"), swap_near(gain_sum, "dp"), final, expert_grads)
    )
    by_dp = total(by_dp)
    qkv_grad = by_dp[:, : 3 * head_width].reshape(feats, 3, head_width).transpose(1, 0, 2)
    out_grad = by_dp[:, 3 * head_width : 4 * head_width].T
    tail = by_dp[:, 4 * head_width :]
    router_grad = tail[:, :experts].T
    gain_second_grad = tail[:, experts] + tail[:, experts + 1]
    gain_first_grad = total(gain_sum)[0]

    return (
        final[:, :part],
        final[:, part:],
        qkv_grad,
        out_grad,
        router_grad,
        *expert_grads,
        gain_first_grad,
        gain_second_grad,
    )


def solution(mesh):
    sizes = mesh.shape
    split = Mesh(
        mesh.devices.reshape(sizes["dp"], sizes["expert"] // 2, 2, sizes["tensor"]),
        ("dp", "z", "core", "tensor"),
    )
    experts = ("z", "core")
    every = ("dp", "z", "core")
    placed = (
        P(every, None),
        P(every, None),
        P(every, None),
        P(every),
        P(every, None),
        P(every, None),
        P(None, every, "tensor"),
        P("tensor", every),
        P(None, every),
        P(experts, "dp", "tensor"),
        P(experts, "dp", "tensor"),
        P(experts, "dp", "tensor"),
        P(),
        P(),
    )
    return jax.shard_map(
        local,
        mesh=split,
        in_specs=placed,
        out_specs=(
            P(every, "tensor"),
            P(every, "tensor"),
            P(None, every, "tensor"),
            P("tensor", every),
            P(None, every),
            P(experts, "dp", "tensor"),
            P(experts, "dp", "tensor"),
            P(experts, "dp", "tensor"),
            P(every),
            P(every),
        ),
        check_vma=False,
    )
```

profile of v0, /device:TPU:0, one launch (start us, length us, event | category | flops | bytes accessed | tf_op | source)
XLA Modules:
  0.0 336.3 jit_solution(158427821393391195)
XLA Ops:
  16.5 3.6 %collective-permute-start.1 = (bf16[128,640]{0,1:T(8,128)(2,1)S(1)}, bf16[128,640]{0,1:T(8,128)(2,1)S(1)}, u32[]{:S(2)}, u32[]{:S(2)}) collective-permute-start(bf16[128,640]{0,1:T(8,128)(2,1)S(1)} %pad_maximum_fusion.10), channel_id=1, source_target_pairs={{0,16},{8,24},{16,0},{24,8},{1,17},{9,25},{17,1},{25,9},{2,18},{10... | collective-permute-start | bytes 491528 | tf_op jit(solution)/shard_map/ppermute | solution.py:20
  22.8 4.7 %collective-permute-done.1 = bf16[128,640]{0,1:T(8,128)(2,1)S(1)} collective-permute-done((bf16[128,640]{0,1:T(8,128)(2,1)S(1)}, bf16[128,640]{0,1:T(8,128)(2,1)S(1)}, u32[]{:S(2)}, u32[]{:S(2)}) %collective-permute-start.1) | collective-permute-done | bytes 163872 | tf_op jit(solution)/shard_map/ppermute | solution.py:20
  28.3 4.2 %all-to-all-start = ((bf16[8,16,2048]{2,1,0:T(8,128)(2,1)}), bf16[8,16,2048]{2,1,0:T(8,128)(2,1)S(1)}, u32[]{:S(2)}, u32[]{:S(2)}) async-start(bf16[8,16,2048]{2,1,0:T(8,128)(2,1)} %bitcast.7), calls=%async_computation | async-start | bytes 1048576 | tf_op jit(solution)/shard_map/all_to_all | solution.py:820
  32.5 2.9 collective-permute-start.7
  38.1 3.0 collective-permute-start.4
  47.2 3.4 %collective-permute-done.7.w1 = bf16[2,512,256]{2,1,0:T(8,128)(2,1)} collective-permute-done((bf16[2,512,256]{2,1,0:T(8,128)(2,1)}, bf16[2,512,256]{2,1,0:T(8,128)(2,1)}, u32[]{:S(2)}, u32[]{:S(2)}) %collective-permute-start.7) | collective-permute-done | bytes 524320 | tf_op jit(solution)/shard_map/ppermute | solution.py:20
  50.5 4.6 %all-to-all-start.1 = ((bf16[8,128,256]{2,1,0:T(8,128)(2,1)}), bf16[8,128,256]{2,1,0:T(8,128)(2,1)S(1)}, u32[]{:S(2)}, u32[]{:S(2)}) async-start(bf16[8,128,256]{2,1,0:T(8,128)(2,1)} %get-tuple-element.136), calls=%async_computation.1 | async-start | bytes 1048576 | tf_op jit(solution)/shard_map/all_to_all | solution.py:828
  56.4 3.9 %collective-permute-start.10 = (bf16[1,512,256]{2,1,0:T(8,128)(2,1)S(1)}, bf16[1,512,256]{2,1,0:T(8,128)(2,1)}, u32[]{:S(2)}, u32[]{:S(2)}) collective-permute-start(bf16[1,512,256]{2,1,0:T(8,128)(2,1)S(1)} %slice.122), channel_id=1, source_target_pairs={{0,96},{32,0},{64,32},{96,64},{1,97},{33,1},{65,33},{97,65},{2,98}... | collective-permute-start | bytes 786440 | tf_op jit(solution)/shard_map/ppermute | solution.py:20
  67.4 3.5 %collective-permute-done.10 = bf16[1,512,256]{2,1,0:T(8,128)(2,1)} collective-permute-done((bf16[1,512,256]{2,1,0:T(8,128)(2,1)S(1)}, bf16[1,512,256]{2,1,0:T(8,128)(2,1)}, u32[]{:S(2)}, u32[]{:S(2)}) %collective-permute-start.10) | collective-permute-done | bytes 262176 | tf_op jit(solution)/shard_map/ppermute | solution.py:20
  70.9 3.5 %collective-permute-done.9 = bf16[1,512,256]{2,1,0:T(8,128)(2,1)} collective-permute-done((bf16[1,512,256]{2,1,0:T(8,128)(2,1)}, bf16[1,512,256]{2,1,0:T(8,128)(2,1)}, u32[]{:S(2)}, u32[]{:S(2)}) %collective-permute-start.9) | collective-permute-done | bytes 262176 | tf_op jit(solution)/shard_map/ppermute | solution.py:20
  78.0 6.9 %attention.1 = (bf16[3,128,512]{2,1,0:T(8,128)(2,1)}, f32[4,128,128]{2,1,0:T(8,128)}, bf16[128,512]{1,0:T(8,128)(2,1)}, bf16[128,512]{1,0:T(8,128)(2,1)}, bf16[1...) custom-call(s32[3]{0:T(128)} %pad_add_fusion.where, ...), custom_call_target="tpu_custom_call" | custom-call | flops 2000000000 | bytes 10000000 | tf_op jit(solution)/shard_map/attention/pallas_call | solution.py:162
  84.9 15.9 %collective-permute-start.13 = (bf16[128,512]{1,0:T(8,128)(2,1)}, bf16[128,512]{1,0:T(8,128)(2,1)S(1)}, u32[]{:S(2)}, u32[]{:S(2)}) collective-permute-start(bf16[128,512]{1,0:T(8,128)(2,1)} %get-tuple-element.144), channel_id=1, source_target_pairs={{0,2},{1,3},{2,0},{3,1},{4,6},{5,7},{6,4},{7,5},{8,10},{9,11},{10,... | collective-permute-start | bytes 393224 | tf_op jit(solution)/shard_map/ppermute | solution.py:20
  105.6 2.9 collective-permute-done.12
  116.1 4.0 %collective-permute-done.15 = bf16[128,512]{1,0:T(8,128)(2,1)S(1)} collective-permute-done((bf16[128,512]{1,0:T(8,128)(2,1)S(1)}, bf16[128,512]{1,0:T(8,128)(2,1)S(1)}, u32[]{:S(2)}, u32[]{:S(2)}) %collective-permute-start.15) | collective-permute-done | bytes 131104 | tf_op jit(solution)/shard_map/ppermute | solution.py:20
  123.5 8.3 %back.1 = (bf16[1024,2048]{1,0:T(8,128)(2,1)}, f32[1024,512]{1,0:T(8,128)}, bf16[128,2048]{1,0:T(8,128)(2,1)}, bf16[2,2048,256]{2,1,0:T(8,128)(2,1)}) custom-call(s32[3]{0:T(128)} %pad_add_fusion.where, bf16[4,512,512]{2,1,0:T(8,128)(2,1)} %pad_maximum_fusion.g_own, bf16[4,512,512]{2,1,0:T(8,128)(2,1)} %collective-permute-done.17.g_other, ...), custom_call_target="tpu_custom_call" | custom-call | flops 2000000000 | bytes 13000000 | tf_op jit(solution)/shard_map/back/pallas_call | solution.py:539
  141.5 6.7 %collective-permute-done.20 = bf16[2,128,512]{2,1,0:T(8,128)(2,1)S(1)} collective-permute-done((bf16[2,128,512]{2,1,0:T(8,128)(2,1)S(1)}, bf16[2,128,512]{2,1,0:T(8,128)(2,1)S(1)}, u32[]{:S(2)}, u32[]{:S(2)}) %collective-permute-start.20) | collective-permute-done | bytes 262176 | tf_op jit(solution)/shard_map/ppermute | solution.py:20
  152.1 21.0 %experts.1 = (bf16[4,4,144,512]{3,2,1,0:T(8,128)(2,1)}, bf16[4,4,144,512]{3,2,1,0:T(8,128)(2,1)}, bf16[1024,2048]{1,0:T(8,128)(2,1)}, bf16[3,1024,512]{2,1,0:T(8...) custom-call(s32[3]{0:T(128)} %pad_add_fusion.where, bf16[3,4,128,512]{3,2,1,0:T(8,128)(2,1)} %copy-done.8, ...), custom_call_target="tpu_custom_call" | custom-call | flops 8999999488 | bytes 26000000 | tf_op jit(solution)/shard_map/experts/pallas_call | solution.py:671
  173.3 5.9 %rows.1 = (bf16[512,2048]{1,0:T(8,128)(2,1)}, bf16[512,2048]{1,0:T(8,128)(2,1)}) custom-call(bf16[3,1024,512]{2,1,0:T(8,128)(2,1)} %get-tuple-element.167.mid, bf16[2,2048,256]{2,1,0:T(8,128)(2,1)} %get-tuple-element.168.w), custom_call_target="tpu_custom_call" | custom-call | flops 2000000000 | bytes 7000000 | tf_op jit(solution)/shard_map/rows/pallas_call | solution.py:744
  179.2 4.3 %pair.2 = (bf16[4,144,512]{2,1,0:T(8,128)(2,1)}, bf16[4,144,512]{2,1,0:T(8,128)(2,1)}, bf16[4,144,512]{2,1,0:T(8,128)(2,1)}, bf16[4,144,512]{2,1,0:T(8,128)(2,1)}) custom-call(bf16[4,4,144,512]{3,2,1,0:T(8,128)(2,1)} %get-tuple-element.161.own, bf16[4,4,144,512]{3,2,1,0:T(8,128)(2,1)} %collective-permute-done.24.other), custom_call_target="tpu_custom_call" | custom-call | flops 1000000 | bytes 7077888 | tf_op jit(solution)/shard_map/pair/pallas_call | solution.py:358
  188.8 4.2 %pair.3 = (bf16[128,2048]{1,0:T(8,128)(2,1)}, bf16[128,2048]{1,0:T(8,128)(2,1)}, bf16[128,2048]{1,0:T(8,128)(2,1)}, bf16[128,2048]{1,0:T(8,128)(2,1)}) custom-call(bf16[4,128,2048]{2,1,0:T(8,128)(2,1)} %bitcast.87, bf16[4,128,2048]{2,1,0:T(8,128)(2,1)} %bitcast.32.other), custom_call_target="tpu_custom_call" | custom-call | flops 1000000 | bytes 6291456 | tf_op jit(solution)/shard_map/pair/pallas_call | solution.py:358
  196.2 4.8 %collective-permute-done.25.p1 = bf16[4,144,512]{2,1,0:T(8,128)(2,1)S(1)} collective-permute-done((bf16[4,144,512]{2,1,0:T(8,128)(2,1)}, bf16[4,144,512]{2,1,0:T(8,128)(2,1)S(1)}, u32[]{:S(2)}, u32[]{:S(2)}) %collective-permute-start.25) | collective-permute-done | bytes 589856 | tf_op jit(solution)/shard_map/ppermute | solution.py:20
  203.8 11.4 %grads.1 = bf16[4,6,512,256]{3,2,1,0:T(8,128)(2,1)} custom-call(bf16[1024,2048]{1,0:T(8,128)(2,1)} %get-tuple-element.181.h.hidden, bf16[1024,2048]{1,0:T(8,128)(2,1)} %get-tuple-element.182.g, bf16[3,1024,512]{2,1,0:T(8,128)(2,1)} %get-tuple-element.167.mid, bf16[1024,512]{1,0:T(8,128)(2,1)} %get-tuple-element.183.by_source), custom_call_target="tpu_custom_call" | custom-call | flops 7000000000 | bytes 18000000 | tf_op jit(solution)/shard_map/grads/pallas_call | solution.py:719
  215.2 6.2 %collective-permute-done.30.p2 = bf16[128,2048]{1,0:T(8,128)(2,1)} collective-permute-done((bf16[128,2048]{1,0:T(8,128)(2,1)}, bf16[128,2048]{1,0:T(8,128)(2,1)}, u32[]{:S(2)}, u32[]{:S(2)}) %collective-permute-start.30) | collective-permute-done | bytes 524320 | tf_op jit(solution)/shard_map/ppermute | solution.py:20
  229.1 3.7 %columns.1 = (bf16[128,512]{1,0:T(8,128)(2,1)}, bf16[128,512]{1,0:T(8,128)(2,1)}, bf16[128,512]{1,0:T(8,128)(2,1)}, bf16[128,512]{1,0:T(8,128)(2,1)}) custom-call(s32[3]{0:T(128)} %pad_add_fusion.where, bf16[128,2048]{1,0:T(8,128)(2,1)} %get-tuple-element.200.p0, bf16[128,2048]{1,0:T(8,128)(2,1)} %collective-permute-done.29.p1, ...), custom_call_target="tpu_custom_call" | custom-call | flops 1000000 | bytes 3000000 | tf_op jit(solution)/shard_map/columns/pallas_call | solution.py:426
  254.2 7.0 %attention_back.1 = (bf16[8,160,256]{2,1,0:T(8,128)(2,1)}, bf16[128,1536]{1,0:T(8,128)(2,1)}, f32[128,512]{1,0:T(8,128)}) custom-call(s32[3]{0:T(128)} %pad_add_fusion.where, bf16[128,512]{1,0:T(8,128)(2,1)} %get-tuple-element.217.g0, bf16[128,512]{1,0:T(8,128)(2,1)} %copy-done.22, bf16[128,512]{1,0:T(8,128)(2,1)} %copy-done.23, ...), custom_call_target="tpu_custom_call" | custom-call | flops 1000000000 | bytes 6000000 | tf_op jit(solution)/shard_map/attention_back/pallas_call | solution.py:260
  266.2 4.2 %all-to-all-start.2 = ((bf16[8,160,256]{2,1,0:T(8,128)(2,1)}), bf16[8,160,256]{2,1,0:T(8,128)(2,1)}, u32[]{:S(2)}, u32[]{:S(2)}) async-start(bf16[8,160,256]{2,1,0:T(8,128)(2,1)} %get-tuple-element.227), calls=%async_computation.2 | async-start | bytes 1310720 | tf_op jit(solution)/shard_map/all_to_all | solution.py:897
  270.4 6.4 %normed_back.1 = (bf16[144,640]{1,0:T(8,128)(2,1)}, bf16[144,640]{1,0:T(8,128)(2,1)}, bf16[144,640]{1,0:T(8,128)(2,1)}, bf16[144,640]{1,0:T(8,128)(2,1)}) custom-call(s32[3]{0:T(128)} %pad_add_fusion.where, bf16[128,1536]{1,0:T(8,128)(2,1)} %get-tuple-element.226.grad_proj, bf16[128,2048]{1,0:T(8,128)(2,1)} %bitcast.82, f32[1,2048]{1,0:T(1,128)} %bitcast.108, ...), custom_call_target="tpu_custom_call" | custom-call | flops 1000000000 | bytes 8000000 | tf_op jit(solution)/shard_map/normed_back/pallas_call | solution.py:336
  286.1 4.1 %collective-permute-done.49 = bf16[144,640]{1,0:T(8,128)(2,1)S(1)} collective-permute-done((bf16[144,640]{1,0:T(8,128)(2,1)}, bf16[144,640]{1,0:T(8,128)(2,1)S(1)}, u32[]{:S(2)}, u32[]{:S(2)}) %collective-permute-start.49) | collective-permute-done | bytes 184352 | tf_op jit(solution)/shard_map/ppermute | solution.py:20
  293.1 4.5 %all-to-all-start.3 = ((bf16[8,32,1024]{2,1,0:T(8,128)(2,1)}), bf16[8,32,1024]{2,1,0:T(8,128)(2,1)S(1)}, u32[]{:S(2)}, u32[]{:S(2)}) async-start(bf16[8,32,1024]{2,1,0:T(8,128)(2,1)} %pad_maximum_fusion.7), calls=%async_computation.3 | async-start | bytes 1048576 | tf_op jit(solution)/shard_map/all_to_all | solution.py:928
  297.6 5.7 %tail.1 = (bf16[64,2176]{1,0:T(8,128)(2,1)}, bf16[64,2176]{1,0:T(8,128)(2,1)}, bf16[64,2176]{1,0:T(8,128)(2,1)}, bf16[64,2176]{1,0:T(8,128)(2,1)}) custom-call(s32[3]{0:T(128)} %pad_add_fusion.where, bf16[8,128,256]{2,1,0:T(8,128)(2,1)} %copy-done.6, bf16[4,128,1536]{2,1,0:T(8,128)(2,1)} %copy-done.4, bf16[4,128,1536]{2,1,0:T(8,128)(2,1)} %collective-permute-done.44.other, ...), custom_call_target="tpu_custom_call" | custom-call | flops 1000000000 | bytes 8000000 | tf_op jit(solution)/shard_map/tail/pallas_call | solution.py:465
  311.6 8.3 %collective-permute-done.51 = f32[1,64]{1,0:T(1,128)S(1)} collective-permute-done((f32[1,64]{1,0:T(1,128)S(1)}, f32[1,64]{1,0:T(1,128)S(1)}, u32[]{:S(2)}, u32[]{:S(2)}) %collective-permute-start.51) | collective-permute-done | bytes 288 | tf_op jit(solution)/shard_map/ppermute | solution.py:20
  319.9 3.1 fusion
  (250 shorter events, 135.1 us)
Async XLA Ops:
  7.2 69.1 %all-gather.4.cloned.1.call-start = ((), (), s32[]{:S(2)}) async-start(), calls=%async_computation.5 | async-start | bytes 9191424 | tf_op jit(solution)/shard_map/all_gather | solution.py:796
  28.3 14.9 %all-to-all-start = ((bf16[8,16,2048]{2,1,0:T(8,128)(2,1)}), bf16[8,16,2048]{2,1,0:T(8,128)(2,1)S(1)}, u32[]{:S(2)}, u32[]{:S(2)}) async-start(bf16[8,16,2048]{2,1,0:T(8,128)(2,1)} %bitcast.7), calls=%async_computation | async-start | bytes 1048576 | tf_op jit(solution)/shard_map/all_to_all | solution.py:820
  32.5 117.6 %all-gather.6.cloned.1.call-start = ((), (), s32[]{:S(2)}) async-start(), calls=%async_computation.6 | async-start | bytes 5242880 | tf_op jit(solution)/shard_map/all_gather | solution.py:830
  32.5 18.0 %collective-permute-start.7 = (bf16[2,512,256]{2,1,0:T(8,128)(2,1)}, bf16[2,512,256]{2,1,0:T(8,128)(2,1)}, u32[]{:S(2)}, u32[]{:S(2)}) collective-permute-start(bf16[2,512,256]{2,1,0:T(8,128)(2,1)} %w0), channel_id=1, source_target_pairs={{0,96},{32,0},{64,32},{96,64},{1,97},{33,1},{65,33},{97,65},{2,98}... | collective-permute-start | bytes 1572872 | tf_op jit(solution)/shard_map/ppermute | solution.py:20
  35.4 21.0 %collective-permute-start.8 = (bf16[2,512,256]{2,1,0:T(8,128)(2,1)}, bf16[2,512,256]{2,1,0:T(8,128)(2,1)}, u32[]{:S(2)}, u32[]{:S(2)}) collective-permute-start(bf16[2,512,256]{2,1,0:T(8,128)(2,1)} %w0), channel_id=1, source_target_pairs={{0,32},{32,64},{64,96},{96,0},{1,33},{33,65},{65,97},{97,1},{2,34}... | collective-permute-start | bytes 1572872 | tf_op jit(solution)/shard_map/ppermute | solution.py:20
  36.5 26.4 %collective-permute-start.5 = (bf16[4,128,512]{1,2,0:T(8,128)(2,1)S(1)}, bf16[4,128,512]{1,2,0:T(8,128)(2,1)}, u32[]{:S(2)}, u32[]{:S(2)}) collective-permute-start(bf16[4,128,512]{1,2,0:T(8,128)(2,1)S(1)} %pad_maximum_fusion.4), channel_id=1, source_target_pairs={{0,1},{1,2},{2,3},{3,0},{4,5},{5,6},{6,7},{7,4},{8,9},{9,10},{10,1... | collective-permute-start | bytes 1572872 | tf_op jit(solution)/shard_map/ppermute | solution.py:20
  38.1 26.2 %collective-permute-start.4 = (bf16[4,128,512]{1,2,0:T(8,128)(2,1)S(1)}, bf16[4,128,512]{1,2,0:T(8,128)(2,1)}, u32[]{:S(2)}, u32[]{:S(2)}) collective-permute-start(bf16[4,128,512]{1,2,0:T(8,128)(2,1)S(1)} %pad_maximum_fusion.4), channel_id=1, source_target_pairs={{0,2},{1,3},{2,0},{3,1},{4,6},{5,7},{6,4},{7,5},{8,10},{9,11},{10,... | collective-permute-start | bytes 1572872 | tf_op jit(solution)/shard_map/ppermute | solution.py:20
  41.0 24.5 %collective-permute-start.3 = (bf16[4,128,512]{1,2,0:T(8,128)(2,1)S(1)}, bf16[4,128,512]{1,2,0:T(8,128)(2,1)S(1)}, u32[]{:S(2)}, u32[]{:S(2)}) collective-permute-start(bf16[4,128,512]{1,2,0:T(8,128)(2,1)S(1)} %pad_maximum_fusion.4), channel_id=1, source_target_pairs={{0,3},{1,0},{2,1},{3,2},{4,7},{5,4},{6,5},{7,6},{8,11},{9,8},{10,9... | collective-permute-start | bytes 1572872 | tf_op jit(solution)/shard_map/ppermute | solution.py:20
  50.5 25.7 %all-to-all-start.1 = ((bf16[8,128,256]{2,1,0:T(8,128)(2,1)}), bf16[8,128,256]{2,1,0:T(8,128)(2,1)S(1)}, u32[]{:S(2)}, u32[]{:S(2)}) async-start(bf16[8,128,256]{2,1,0:T(8,128)(2,1)} %get-tuple-element.136), calls=%async_computation.1 | async-start | bytes 1048576 | tf_op jit(solution)/shard_map/all_to_all | solution.py:828
  55.1 242.5 %all-gather.8.cloned.1.call-start = ((), (), s32[]{:S(2)}) async-start(), calls=%async_computation.7 | async-start | bytes 1179648 | tf_op jit(solution)/shard_map/all_gather | solution.py:836
  56.4 14.5 %collective-permute-start.10 = (bf16[1,512,256]{2,1,0:T(8,128)(2,1)S(1)}, bf16[1,512,256]{2,1,0:T(8,128)(2,1)}, u32[]{:S(2)}, u32[]{:S(2)}) collective-permute-start(bf16[1,512,256]{2,1,0:T(8,128)(2,1)S(1)} %slice.122), channel_id=1, source_target_pairs={{0,96},{32,0},{64,32},{96,64},{1,97},{33,1},{65,33},{97,65},{2,98}... | collective-permute-start | bytes 786440 | tf_op jit(solution)/shard_map/ppermute | solution.py:20
  76.3 43.9 %collective-permute-start.17 = (bf16[4,512,512]{2,1,0:T(8,128)(2,1)}, bf16[4,512,512]{2,1,0:T(8,128)(2,1)}, u32[]{:S(2)}, u32[]{:S(2)}) collective-permute-start(bf16[4,512,512]{2,1,0:T(8,128)(2,1)} %pad_maximum_fusion.g_own), channel_id=1, source_target_pairs={{0,4},{4,0},{1,5},{5,1},{2,6},{6,2},{3,7},{7,3},{8,12},{12,8},{9,1... | collective-permute-start | bytes 6291464 | tf_op jit(solution)/shard_map/ppermute | solution.py:24
  84.9 20.7 %collective-permute-start.13 = (bf16[128,512]{1,0:T(8,128)(2,1)}, bf16[128,512]{1,0:T(8,128)(2,1)S(1)}, u32[]{:S(2)}, u32[]{:S(2)}) collective-permute-start(bf16[128,512]{1,0:T(8,128)(2,1)} %get-tuple-element.144), channel_id=1, source_target_pairs={{0,2},{1,3},{2,0},{3,1},{4,6},{5,7},{6,4},{7,5},{8,10},{9,11},{10,... | collective-permute-start | bytes 393224 | tf_op jit(solution)/shard_map/ppermute | solution.py:20
  120.2 14.4 %collective-permute-start.18 = (bf16[4,128,512]{2,1,0:T(8,128)(2,1)S(1)}, bf16[4,128,512]{2,1,0:T(8,128)(2,1)S(1)}, u32[]{:S(2)}, u32[]{:S(2)}) collective-permute-start(bf16[4,128,512]{2,1,0:T(8,128)(2,1)S(1)} %pad_maximum_fusion.6.resid), channel_id=1, source_target_pairs={{0,8},{8,16},{16,24},{24,0},{1,9},{9,17},{17,25},{25,1},{2,10},{10... | collective-permute-start | bytes 1572872 | tf_op jit(solution)/shard_map/ppermute | solution.py:20
  121.9 13.0 %collective-permute-start.19 = (bf16[4,128,512]{2,1,0:T(8,128)(2,1)S(1)}, bf16[4,128,512]{2,1,0:T(8,128)(2,1)}, u32[]{:S(2)}, u32[]{:S(2)}) collective-permute-start(bf16[4,128,512]{2,1,0:T(8,128)(2,1)S(1)} %pad_maximum_fusion.6.resid), channel_id=1, source_target_pairs={{0,24},{8,0},{16,8},{24,16},{1,25},{9,1},{17,9},{25,17},{2,26},{10... | collective-permute-start | bytes 1572872 | tf_op jit(solution)/shard_map/ppermute | solution.py:20
  183.9 136.0 %reduce-scatter.2.cloned.1.call-start = ((), (), s32[]{:S(2)}) async-start(), calls=%async_computation.8 | async-start | bytes 7864320 | tf_op jit(solution)/shard_map/reduce_scatter | solution.py:921
  183.9 17.0 %collective-permute-start.25 = (bf16[4,144,512]{2,1,0:T(8,128)(2,1)}, bf16[4,144,512]{2,1,0:T(8,128)(2,1)S(1)}, u32[]{:S(2)}, u32[]{:S(2)}) collective-permute-start(bf16[4,144,512]{2,1,0:T(8,128)(2,1)} %get-tuple-element.172), channel_id=1, source_target_pairs={{0,1},{1,2},{2,3},{3,0},{4,5},{5,6},{6,7},{7,4},{8,9},{9,10},{10,1... | collective-permute-start | bytes 1769480 | tf_op jit(solution)/shard_map/ppermute | solution.py:20
  185.3 29.8 %collective-permute-start.26 = (bf16[4,144,512]{2,1,0:T(8,128)(2,1)}, bf16[4,144,512]{2,1,0:T(8,128)(2,1)S(1)}, u32[]{:S(2)}, u32[]{:S(2)}) collective-permute-start(bf16[4,144,512]{2,1,0:T(8,128)(2,1)} %get-tuple-element.173), channel_id=1, source_target_pairs={{0,3},{1,0},{2,1},{3,2},{4,7},{5,4},{6,5},{7,6},{8,11},{9,8},{10,9... | collective-permute-start | bytes 1769480 | tf_op jit(solution)/shard_map/ppermute | solution.py:20
  187.2 27.9 %collective-permute-start.27 = (bf16[4,144,512]{2,1,0:T(8,128)(2,1)}, bf16[4,144,512]{2,1,0:T(8,128)(2,1)}, u32[]{:S(2)}, u32[]{:S(2)}) collective-permute-start(bf16[4,144,512]{2,1,0:T(8,128)(2,1)} %get-tuple-element.174), channel_id=1, source_target_pairs={{0,2},{1,3},{2,0},{3,1},{4,6},{5,7},{6,4},{7,5},{8,10},{9,11},{10,... | collective-permute-start | bytes 1769480 | tf_op jit(solution)/shard_map/ppermute | solution.py:20
  193.0 22.2 %collective-permute-start.29 = (bf16[128,2048]{1,0:T(8,128)(2,1)}, bf16[128,2048]{1,0:T(8,128)(2,1)}, u32[]{:S(2)}, u32[]{:S(2)}) collective-permute-start(bf16[128,2048]{1,0:T(8,128)(2,1)} %get-tuple-element.178), channel_id=1, source_target_pairs={{0,8},{8,16},{16,24},{24,0},{1,9},{9,17},{17,25},{25,1},{2,10},{10... | collective-permute-start | bytes 1572872 | tf_op jit(solution)/shard_map/ppermute | solution.py:20
  194.1 27.2 %collective-permute-start.30 = (bf16[128,2048]{1,0:T(8,128)(2,1)}, bf16[128,2048]{1,0:T(8,128)(2,1)}, u32[]{:S(2)}, u32[]{:S(2)}) collective-permute-start(bf16[128,2048]{1,0:T(8,128)(2,1)} %get-tuple-element.179), channel_id=1, source_target_pairs={{0,24},{8,0},{16,8},{24,16},{1,25},{9,1},{17,9},{25,17},{2,26},{10... | collective-permute-start | bytes 1572872 | tf_op jit(solution)/shard_map/ppermute | solution.py:20
  201.0 22.0 %collective-permute-start.31 = (bf16[128,2048]{1,0:T(8,128)(2,1)}, bf16[128,2048]{1,0:T(8,128)(2,1)}, u32[]{:S(2)}, u32[]{:S(2)}) collective-permute-start(bf16[128,2048]{1,0:T(8,128)(2,1)} %get-tuple-element.180), channel_id=1, source_target_pairs={{0,16},{8,24},{16,0},{24,8},{1,17},{9,25},{17,1},{25,9},{2,18},{10... | collective-permute-start | bytes 1572872 | tf_op jit(solution)/shard_map/ppermute | solution.py:20
  261.2 19.2 %collective-permute-start.43 = (bf16[128,1536]{1,0:T(8,128)(2,1)}, bf16[128,1536]{1,0:T(8,128)(2,1)S(1)}, u32[]{:S(2)}, u32[]{:S(2)}) collective-permute-start(bf16[128,1536]{1,0:T(8,128)(2,1)} %get-tuple-element.226.grad_proj), channel_id=1, source_target_pairs={{0,8},{8,16},{16,24},{24,0},{1,9},{9,17},{17,25},{25,1},{2,10},{10... | collective-permute-start | bytes 1179656 | tf_op jit(solution)/shard_map/ppermute | solution.py:20
  263.0 19.5 %collective-permute-start.42 = (bf16[128,1536]{1,0:T(8,128)(2,1)}, bf16[128,1536]{1,0:T(8,128)(2,1)S(1)}, u32[]{:S(2)}, u32[]{:S(2)}) collective-permute-start(bf16[128,1536]{1,0:T(8,128)(2,1)} %get-tuple-element.226.grad_proj), channel_id=1, source_target_pairs={{0,16},{8,24},{16,0},{24,8},{1,17},{9,25},{17,1},{25,9},{2,18},{10... | collective-permute-start | bytes 1179656 | tf_op jit(solution)/shard_map/ppermute | solution.py:20
  265.1 17.7 %collective-permute-start.41 = (bf16[128,1536]{1,0:T(8,128)(2,1)}, bf16[128,1536]{1,0:T(8,128)(2,1)}, u32[]{:S(2)}, u32[]{:S(2)}) collective-permute-start(bf16[128,1536]{1,0:T(8,128)(2,1)} %get-tuple-element.226.grad_proj), channel_id=1, source_target_pairs={{0,24},{8,0},{16,8},{24,16},{1,25},{9,1},{17,9},{25,17},{2,26},{10... | collective-permute-start | bytes 1179656 | tf_op jit(solution)/shard_map/ppermute | solution.py:20
  266.2 26.9 %all-to-all-start.2 = ((bf16[8,160,256]{2,1,0:T(8,128)(2,1)}), bf16[8,160,256]{2,1,0:T(8,128)(2,1)}, u32[]{:S(2)}, u32[]{:S(2)}) async-start(bf16[8,160,256]{2,1,0:T(8,128)(2,1)} %get-tuple-element.227), calls=%async_computation.2 | async-start | bytes 1310720 | tf_op jit(solution)/shard_map/all_to_all | solution.py:897
  284.1 13.5 %collective-permute-start.44 = (bf16[4,128,1536]{2,1,0:T(8,128)(2,1)S(1)}, bf16[4,128,1536]{2,1,0:T(8,128)(2,1)}, u32[]{:S(2)}, u32[]{:S(2)}) collective-permute-start(bf16[4,128,1536]{2,1,0:T(8,128)(2,1)S(1)} %pad_maximum_fusion.2.own), channel_id=1, source_target_pairs={{0,4},{4,0},{1,5},{5,1},{2,6},{6,2},{3,7},{7,3},{8,12},{12,8},{9,1... | collective-permute-start | bytes 4718600 | tf_op jit(solution)/shard_map/ppermute | solution.py:24
  293.1 14.8 %all-to-all-start.3 = ((bf16[8,32,1024]{2,1,0:T(8,128)(2,1)}), bf16[8,32,1024]{2,1,0:T(8,128)(2,1)S(1)}, u32[]{:S(2)}, u32[]{:S(2)}) async-start(bf16[8,32,1024]{2,1,0:T(8,128)(2,1)} %pad_maximum_fusion.7), calls=%async_computation.3 | async-start | bytes 1048576 | tf_op jit(solution)/shard_map/all_to_all | solution.py:928
  303.3 21.6 %collective-permute-start.45 = (bf16[64,2176]{1,0:T(8,128)(2,1)}, bf16[64,2176]{1,0:T(8,128)(2,1)S(1)}, u32[]{:S(2)}, u32[]{:S(2)}) collective-permute-start(bf16[64,2176]{1,0:T(8,128)(2,1)} %get-tuple-element.230), channel_id=1, source_target_pairs={{0,32},{32,64},{64,96},{96,0},{1,33},{33,65},{65,97},{97,1},{2,34}... | collective-permute-start | bytes 835592 | tf_op jit(solution)/shard_map/ppermute | solution.py:20
  303.9 21.0 %collective-permute-start.46 = (bf16[64,2176]{1,0:T(8,128)(2,1)}, bf16[64,2176]{1,0:T(8,128)(2,1)S(1)}, u32[]{:S(2)}, u32[]{:S(2)}) collective-permute-start(bf16[64,2176]{1,0:T(8,128)(2,1)} %get-tuple-element.231), channel_id=1, source_target_pairs={{0,96},{32,0},{64,32},{96,64},{1,97},{33,1},{65,33},{97,65},{2,98}... | collective-permute-start | bytes 835592 | tf_op jit(solution)/shard_map/ppermute | solution.py:20
  306.6 18.3 %collective-permute-start.47 = (bf16[64,2176]{1,0:T(8,128)(2,1)}, bf16[64,2176]{1,0:T(8,128)(2,1)S(1)}, u32[]{:S(2)}, u32[]{:S(2)}) collective-permute-start(bf16[64,2176]{1,0:T(8,128)(2,1)} %get-tuple-element.232), channel_id=1, source_target_pairs={{0,64},{32,96},{64,0},{96,32},{1,65},{33,97},{65,1},{97,33},{2,66}... | collective-permute-start | bytes 835592 | tf_op jit(solution)/shard_map/ppermute | solution.py:20
  308.6 14.5 %collective-permute-start.52 = (f32[1,64]{1,0:T(1,128)S(1)}, f32[1,64]{1,0:T(1,128)S(1)}, u32[]{:S(2)}, u32[]{:S(2)}) collective-permute-start(f32[1,64]{1,0:T(1,128)S(1)} %get-tuple-element.310), channel_id=1, source_target_pairs={{0,96},{32,0},{64,32},{96,64},{1,97},{33,1},{65,33},{97,65},{2,98}... | collective-permute-start | bytes 776 | tf_op jit(solution)/shard_map/ppermute | solution.py:20
  (63 other events, 533.5 us)
Sparse Core Ops, SparseCore 0:
  10.9 63.5 all-gather.3
  76.7 47.6 all-gather.5
  184.0 22.9 all-gather.7
  223.1 62.3 reduce-scatter.1
where the time goes:
time: 340 us; the launch traced here: 336 us
  starting transfers between devices  106 us (31%)
  Pallas kernels  93.5 us (28%)
  waiting for transfers between devices  80.5 us (24%)
  other arithmetic  21.1 us (6%)
  local copies, waits for them, and re-layouts  18.1 us (5%)
  between operations  14.6 us (4%)
    ppermute x47, starting transfers between devices, shift(): lax.ppermute(values, axis, [(i, (i + step) % size) for i in range(size)])  87.5 us
    ppermute x47, waiting for transfers between devices, shift(): lax.ppermute(values, axis, [(i, (i + step) % size) for i in range(size)])  77.4 us
    pallas_call x1, Pallas kernels, experts_call(): pl.pallas_call(expert_kernel, out_shape=(shape((4, 4, 144, 512), BF16), s...  21 us
    pallas_call x1, Pallas kernels, grads_call(): pl.pallas_call(grads_kernel, grid=(4,), out_shape=jax.ShapeDtypeStruct((4...  11.4 us
    pallas_call x2, Pallas kernels, pair_call(): pl.pallas_call(pair_kernel, out_shape=(jax.ShapeDtypeStruct(shape, BF16),...  8.55 us
    pallas_call x1, Pallas kernels, back_call(): pl.pallas_call(back_kernel, out_shape=(shape((1024, 2048), BF16), shape((...  8.28 us
    pallas_call x1, Pallas kernels, attention_back_call(): pl.pallas_call(attention_back_kernel, out_shape=(shape((8, 160, 256), BF1...  6.97 us
    pallas_call x1, Pallas kernels, attention_call(): pl.pallas_call(attention_kernel, out_shape=(shape((3, 128, 512), BF16), s...  6.95 us
  transfers between devices with their start and end apart: 62, of which 34 were waited for; matrix products, arithmetic and copies ran while one was open for 10% of the time, Pallas kernels for 20%

commit v1 on v0

--- a/solution.py
+++ b/solution.py
@@ -875,8 +875,9 @@
         (swap_near(cols, "z"), columns_call(place_now, expert_rows))
     )
     cols, dots = finish_call(cols)
-    grads_near, expert_rows = lax.optimization_barrier(
-        (gather_near(cols, "tensor"), swap_near(expert_rows, "tensor"))
+    expert_rows = swap_near(expert_rows, "tensor")
+    grads_near, expert_rows[:3] = lax.optimization_barrier(
+        (gather_near(cols, "tensor"), expert_rows[:3])
     )
 
     branch_feat, grad_proj, grad_own = attention_back_call(

time: 340 us -> 336 us (0.988)
  waiting for transfers between devices: 80.5 us -> 73.8 us
    ppermute x47, waiting for transfers between devices: 77.4 us -> 71 us  [shift(): lax.ppermute(values, axis, [(i, (i + step) % size) for i in range(size)])]
  transfers between devices with their start and end apart: 62 -> 62, of which waited for: 34 -> 32; matrix products, arithmetic and copies ran while one was open for 10% -> 10% of each run, Pallas kernels for 20% -> 20%
where the time goes in v1:
time: 336 us; the launch traced here: 332 us
  starting transfers between devices  108 us (32%)
  Pallas kernels  93.4 us (28%)
  waiting for transfers between devices  73.8 us (22%)
  other arithmetic  21.1 us (6%)
  local copies, waits for them, and re-layouts  18.1 us (5%)
  between operations  14.6 us (4%)
    ppermute x47, starting transfers between devices, shift(): lax.ppermute(values, axis, [(i, (i + step) % size) for i in range(size)])  90.3 us
    ppermute x47, waiting for transfers between devices, shift(): lax.ppermute(values, axis, [(i, (i + step) % size) for i in range(size)])  71 us
    pallas_call x1, Pallas kernels, experts_call(): pl.pallas_call(expert_kernel, out_shape=(shape((4, 4, 144, 512), BF16), s...  20.9 us
    pallas_call x1, Pallas kernels, grads_call(): pl.pallas_call(grads_kernel, grid=(4,), out_shape=jax.ShapeDtypeStruct((4...  11.4 us
    pallas_call x2, Pallas kernels, pair_call(): pl.pallas_call(pair_kernel, out_shape=(jax.ShapeDtypeStruct(shape, BF16),...  8.52 us
    pallas_call x1, Pallas kernels, back_call(): pl.pallas_call(back_kernel, out_shape=(shape((1024, 2048), BF16), shape((...  8.28 us
    pallas_call x1, Pallas kernels, attention_call(): pl.pallas_call(attention_kernel, out_shape=(shape((3, 128, 512), BF16), s...  6.93 us
    pallas_call x1, Pallas kernels, attention_back_call(): pl.pallas_call(attention_back_kernel, out_shape=(shape((8, 160, 256), BF1...  6.88 us
  transfers between devices with their start and end apart: 62, of which 32 were waited for; matrix products, arithmetic and copies ran while one was open for 10% of the time, Pallas kernels for 20%

profile of v1, /device:TPU:0, one launch (start us, length us, event | category | flops | bytes accessed | tf_op | source)
XLA Modules:
  0.0 331.6 jit_solution(9612442356607021248)
XLA Ops:
  16.5 3.6 %collective-permute-start.1 = (bf16[128,640]{0,1:T(8,128)(2,1)S(1)}, bf16[128,640]{0,1:T(8,128)(2,1)S(1)}, u32[]{:S(2)}, u32[]{:S(2)}) collective-permute-start(bf16[128,640]{0,1:T(8,128)(2,1)S(1)} %pad_maximum_fusion.10), channel_id=1, source_target_pairs={{0,16},{8,24},{16,0},{24,8},{1,17},{9,25},{17,1},{25,9},{2,18},{10... | collective-permute-start | bytes 491528 | tf_op jit(solution)/shard_map/ppermute | solution.py:20
  22.8 4.7 %collective-permute-done.1 = bf16[128,640]{0,1:T(8,128)(2,1)S(1)} collective-permute-done((bf16[128,640]{0,1:T(8,128)(2,1)S(1)}, bf16[128,640]{0,1:T(8,128)(2,1)S(1)}, u32[]{:S(2)}, u32[]{:S(2)}) %collective-permute-start.1) | collective-permute-done | bytes 163872 | tf_op jit(solution)/shard_map/ppermute | solution.py:20
  28.3 4.2 %all-to-all-start = ((bf16[8,16,2048]{2,1,0:T(8,128)(2,1)}), bf16[8,16,2048]{2,1,0:T(8,128)(2,1)S(1)}, u32[]{:S(2)}, u32[]{:S(2)}) async-start(bf16[8,16,2048]{2,1,0:T(8,128)(2,1)} %bitcast.7), calls=%async_computation | async-start | bytes 1048576 | tf_op jit(solution)/shard_map/all_to_all | solution.py:820
  32.5 2.9 collective-permute-start.7
  38.1 3.0 collective-permute-start.4
  47.2 3.4 %collective-permute-done.7.w1 = bf16[2,512,256]{2,1,0:T(8,128)(2,1)} collective-permute-done((bf16[2,512,256]{2,1,0:T(8,128)(2,1)}, bf16[2,512,256]{2,1,0:T(8,128)(2,1)}, u32[]{:S(2)}, u32[]{:S(2)}) %collective-permute-start.7) | collective-permute-done | bytes 524320 | tf_op jit(solution)/shard_map/ppermute | solution.py:20
  50.5 4.6 %all-to-all-start.1 = ((bf16[8,128,256]{2,1,0:T(8,128)(2,1)}), bf16[8,128,256]{2,1,0:T(8,128)(2,1)S(1)}, u32[]{:S(2)}, u32[]{:S(2)}) async-start(bf16[8,128,256]{2,1,0:T(8,128)(2,1)} %get-tuple-element.135), calls=%async_computation.1 | async-start | bytes 1048576 | tf_op jit(solution)/shard_map/all_to_all | solution.py:828
  56.4 3.9 %collective-permute-start.10 = (bf16[1,512,256]{2,1,0:T(8,128)(2,1)S(1)}, bf16[1,512,256]{2,1,0:T(8,128)(2,1)}, u32[]{:S(2)}, u32[]{:S(2)}) collective-permute-start(bf16[1,512,256]{2,1,0:T(8,128)(2,1)S(1)} %slice.122), channel_id=1, source_target_pairs={{0,96},{32,0},{64,32},{96,64},{1,97},{33,1},{65,33},{97,65},{2,98}... | collective-permute-start | bytes 786440 | tf_op jit(solution)/shard_map/ppermute | solution.py:20
  67.4 3.5 %collective-permute-done.10 = bf16[1,512,256]{2,1,0:T(8,128)(2,1)} collective-permute-done((bf16[1,512,256]{2,1,0:T(8,128)(2,1)S(1)}, bf16[1,512,256]{2,1,0:T(8,128)(2,1)}, u32[]{:S(2)}, u32[]{:S(2)}) %collective-permute-start.10) | collective-permute-done | bytes 262176 | tf_op jit(solution)/shard_map/ppermute | solution.py:20
  70.9 3.5 %collective-permute-done.9 = bf16[1,512,256]{2,1,0:T(8,128)(2,1)} collective-permute-done((bf16[1,512,256]{2,1,0:T(8,128)(2,1)}, bf16[1,512,256]{2,1,0:T(8,128)(2,1)}, u32[]{:S(2)}, u32[]{:S(2)}) %collective-permute-start.9) | collective-permute-done | bytes 262176 | tf_op jit(solution)/shard_map/ppermute | solution.py:20
  77.9 6.9 %attention.1 = (bf16[3,128,512]{2,1,0:T(8,128)(2,1)}, f32[4,128,128]{2,1,0:T(8,128)}, bf16[128,512]{1,0:T(8,128)(2,1)}, bf16[128,512]{1,0:T(8,128)(2,1)}, bf16[1...) custom-call(s32[3]{0:T(128)} %pad_add_fusion.where, ...), custom_call_target="tpu_custom_call" | custom-call | flops 2000000000 | bytes 10000000 | tf_op jit(solution)/shard_map/attention/pallas_call | solution.py:162
  84.9 15.9 %collective-permute-start.13 = (bf16[128,512]{1,0:T(8,128)(2,1)}, bf16[128,512]{1,0:T(8,128)(2,1)S(1)}, u32[]{:S(2)}, u32[]{:S(2)}) collective-permute-start(bf16[128,512]{1,0:T(8,128)(2,1)} %get-tuple-element.143), channel_id=1, source_target_pairs={{0,2},{1,3},{2,0},{3,1},{4,6},{5,7},{6,4},{7,5},{8,10},{9,11},{10,... | collective-permute-start | bytes 393224 | tf_op jit(solution)/shard_map/ppermute | solution.py:20
  116.0 4.0 %collective-permute-done.15 = bf16[128,512]{1,0:T(8,128)(2,1)S(1)} collective-permute-done((bf16[128,512]{1,0:T(8,128)(2,1)S(1)}, bf16[128,512]{1,0:T(8,128)(2,1)S(1)}, u32[]{:S(2)}, u32[]{:S(2)}) %collective-permute-start.15) | collective-permute-done | bytes 131104 | tf_op jit(solution)/shard_map/ppermute | solution.py:20
  123.4 8.3 %back.1 = (bf16[1024,2048]{1,0:T(8,128)(2,1)}, f32[1024,512]{1,0:T(8,128)}, bf16[128,2048]{1,0:T(8,128)(2,1)}, bf16[2,2048,256]{2,1,0:T(8,128)(2,1)}) custom-call(s32[3]{0:T(128)} %pad_add_fusion.where, bf16[4,512,512]{2,1,0:T(8,128)(2,1)} %pad_maximum_fusion.g_own, bf16[4,512,512]{2,1,0:T(8,128)(2,1)} %collective-permute-done.17.g_other, ...), custom_call_target="tpu_custom_call" | custom-call | flops 2000000000 | bytes 13000000 | tf_op jit(solution)/shard_map/back/pallas_call | solution.py:539
  141.5 6.7 %collective-permute-done.20 = bf16[2,128,512]{2,1,0:T(8,128)(2,1)S(1)} collective-permute-done((bf16[2,128,512]{2,1,0:T(8,128)(2,1)S(1)}, bf16[2,128,512]{2,1,0:T(8,128)(2,1)S(1)}, u32[]{:S(2)}, u32[]{:S(2)}) %collective-permute-start.20) | collective-permute-done | bytes 262176 | tf_op jit(solution)/shard_map/ppermute | solution.py:20
  152.1 20.9 %experts.1 = (bf16[4,4,144,512]{3,2,1,0:T(8,128)(2,1)}, bf16[4,4,144,512]{3,2,1,0:T(8,128)(2,1)}, bf16[1024,2048]{1,0:T(8,128)(2,1)}, bf16[3,1024,512]{2,1,0:T(8...) custom-call(s32[3]{0:T(128)} %pad_add_fusion.where, bf16[3,4,128,512]{3,2,1,0:T(8,128)(2,1)} %copy-done.8, ...), custom_call_target="tpu_custom_call" | custom-call | flops 8999999488 | bytes 26000000 | tf_op jit(solution)/shard_map/experts/pallas_call | solution.py:671
  173.2 5.8 %rows.1 = (bf16[512,2048]{1,0:T(8,128)(2,1)}, bf16[512,2048]{1,0:T(8,128)(2,1)}) custom-call(bf16[3,1024,512]{2,1,0:T(8,128)(2,1)} %get-tuple-element.166.mid, bf16[2,2048,256]{2,1,0:T(8,128)(2,1)} %get-tuple-element.167.w), custom_call_target="tpu_custom_call" | custom-call | flops 2000000000 | bytes 7000000 | tf_op jit(solution)/shard_map/rows/pallas_call | solution.py:744
  179.1 4.3 %pair.2 = (bf16[4,144,512]{2,1,0:T(8,128)(2,1)}, bf16[4,144,512]{2,1,0:T(8,128)(2,1)}, bf16[4,144,512]{2,1,0:T(8,128)(2,1)}, bf16[4,144,512]{2,1,0:T(8,128)(2,1)}) custom-call(bf16[4,4,144,512]{3,2,1,0:T(8,128)(2,1)} %get-tuple-element.160.own, bf16[4,4,144,512]{3,2,1,0:T(8,128)(2,1)} %collective-permute-done.24.other), custom_call_target="tpu_custom_call" | custom-call | flops 1000000 | bytes 7077888 | tf_op jit(solution)/shard_map/pair/pallas_call | solution.py:358
  188.7 4.2 %pair.3 = (bf16[128,2048]{1,0:T(8,128)(2,1)}, bf16[128,2048]{1,0:T(8,128)(2,1)}, bf16[128,2048]{1,0:T(8,128)(2,1)}, bf16[128,2048]{1,0:T(8,128)(2,1)}) custom-call(bf16[4,128,2048]{2,1,0:T(8,128)(2,1)} %bitcast.87, bf16[4,128,2048]{2,1,0:T(8,128)(2,1)} %bitcast.32.other), custom_call_target="tpu_custom_call" | custom-call | flops 1000000 | bytes 6291456 | tf_op jit(solution)/shard_map/pair/pallas_call | solution.py:358
  196.1 4.8 %collective-permute-done.25.p1 = bf16[4,144,512]{2,1,0:T(8,128)(2,1)S(1)} collective-permute-done((bf16[4,144,512]{2,1,0:T(8,128)(2,1)}, bf16[4,144,512]{2,1,0:T(8,128)(2,1)S(1)}, u32[]{:S(2)}, u32[]{:S(2)}) %collective-permute-start.25) | collective-permute-done | bytes 589856 | tf_op jit(solution)/shard_map/ppermute | solution.py:20
  203.7 11.4 %grads.1 = bf16[4,6,512,256]{3,2,1,0:T(8,128)(2,1)} custom-call(bf16[1024,2048]{1,0:T(8,128)(2,1)} %get-tuple-element.180.h.hidden, bf16[1024,2048]{1,0:T(8,128)(2,1)} %get-tuple-element.181.g, bf16[3,1024,512]{2,1,0:T(8,128)(2,1)} %get-tuple-element.166.mid, bf16[1024,512]{1,0:T(8,128)(2,1)} %get-tuple-element.182.by_source), custom_call_target="tpu_custom_call" | custom-call | flops 7000000000 | bytes 18000000 | tf_op jit(solution)/shard_map/grads/pallas_call | solution.py:719
  215.1 6.1 %collective-permute-done.30.p2 = bf16[128,2048]{1,0:T(8,128)(2,1)} collective-permute-done((bf16[128,2048]{1,0:T(8,128)(2,1)}, bf16[128,2048]{1,0:T(8,128)(2,1)}, u32[]{:S(2)}, u32[]{:S(2)}) %collective-permute-start.30) | collective-permute-done | bytes 524320 | tf_op jit(solution)/shard_map/ppermute | solution.py:20
  229.0 3.8 %columns.1 = (bf16[128,512]{1,0:T(8,128)(2,1)}, bf16[128,512]{1,0:T(8,128)(2,1)}, bf16[128,512]{1,0:T(8,128)(2,1)}, bf16[128,512]{1,0:T(8,128)(2,1)}) custom-call(s32[3]{0:T(128)} %pad_add_fusion.where, bf16[128,2048]{1,0:T(8,128)(2,1)} %get-tuple-element.199.p0, bf16[128,2048]{1,0:T(8,128)(2,1)} %collective-permute-done.29.p1, ...), custom_call_target="tpu_custom_call" | custom-call | flops 1000000 | bytes 3000000 | tf_op jit(solution)/shard_map/columns/pallas_call | solution.py:426
  251.2 6.9 %attention_back.1 = (bf16[8,160,256]{2,1,0:T(8,128)(2,1)}, bf16[128,1536]{1,0:T(8,128)(2,1)}, f32[128,512]{1,0:T(8,128)}) custom-call(s32[3]{0:T(128)} %pad_add_fusion.where, bf16[128,512]{1,0:T(8,128)(2,1)} %get-tuple-element.215.g0, bf16[128,512]{1,0:T(8,128)(2,1)} %copy-done.22, bf16[128,512]{1,0:T(8,128)(2,1)} %copy-done.23, ...), custom_call_target="tpu_custom_call" | custom-call | flops 1000000000 | bytes 6000000 | tf_op jit(solution)/shard_map/attention_back/pallas_call | solution.py:260
  264.0 4.2 %all-to-all-start.2 = ((bf16[8,160,256]{2,1,0:T(8,128)(2,1)}), bf16[8,160,256]{2,1,0:T(8,128)(2,1)}, u32[]{:S(2)}, u32[]{:S(2)}) async-start(bf16[8,160,256]{2,1,0:T(8,128)(2,1)} %get-tuple-element.225), calls=%async_computation.2 | async-start | bytes 1310720 | tf_op jit(solution)/shard_map/all_to_all | solution.py:898
  268.2 6.4 %normed_back.1 = (bf16[144,640]{1,0:T(8,128)(2,1)}, bf16[144,640]{1,0:T(8,128)(2,1)}, bf16[144,640]{1,0:T(8,128)(2,1)}, bf16[144,640]{1,0:T(8,128)(2,1)}) custom-call(s32[3]{0:T(128)} %pad_add_fusion.where, bf16[128,1536]{1,0:T(8,128)(2,1)} %get-tuple-element.224.grad_proj, bf16[128,2048]{1,0:T(8,128)(2,1)} %bitcast.82, f32[1,2048]{1,0:T(1,128)} %bitcast.108, ...), custom_call_target="tpu_custom_call" | custom-call | flops 1000000000 | bytes 8000000 | tf_op jit(solution)/shard_map/normed_back/pallas_call | solution.py:336
  274.6 3.0 collective-permute-start.50
  290.9 3.8 %all-to-all-start.3 = ((bf16[8,32,1024]{2,1,0:T(8,128)(2,1)}), bf16[8,32,1024]{2,1,0:T(8,128)(2,1)S(1)}, u32[]{:S(2)}, u32[]{:S(2)}) async-start(bf16[8,32,1024]{2,1,0:T(8,128)(2,1)} %pad_maximum_fusion.7), calls=%async_computation.3 | async-start | bytes 1048576 | tf_op jit(solution)/shard_map/all_to_all | solution.py:929
  294.7 5.7 %tail.1 = (bf16[64,2176]{1,0:T(8,128)(2,1)}, bf16[64,2176]{1,0:T(8,128)(2,1)}, bf16[64,2176]{1,0:T(8,128)(2,1)}, bf16[64,2176]{1,0:T(8,128)(2,1)}) custom-call(s32[3]{0:T(128)} %pad_add_fusion.where, bf16[8,128,256]{2,1,0:T(8,128)(2,1)} %copy-done.6, bf16[4,128,1536]{2,1,0:T(8,128)(2,1)} %copy-done.4, bf16[4,128,1536]{2,1,0:T(8,128)(2,1)} %collective-permute-done.43.other, ...), custom_call_target="tpu_custom_call" | custom-call | flops 1000000000 | bytes 8000000 | tf_op jit(solution)/shard_map/tail/pallas_call | solution.py:465
  308.7 5.1 %collective-permute-done.51 = f32[1,64]{1,0:T(1,128)S(1)} collective-permute-done((f32[1,64]{1,0:T(1,128)S(1)}, f32[1,64]{1,0:T(1,128)S(1)}, u32[]{:S(2)}, u32[]{:S(2)}) %collective-permute-start.51) | collective-permute-done | bytes 288 | tf_op jit(solution)/shard_map/ppermute | solution.py:20
  313.8 3.3 %collective-permute-start.53 = (f32[1,64]{1,0:T(1,128)S(1)}, f32[1,64]{1,0:T(1,128)S(1)}, u32[]{:S(2)}, u32[]{:S(2)}) collective-permute-start(f32[1,64]{1,0:T(1,128)S(1)} %get-tuple-element.307), channel_id=1, source_target_pairs={{0,64},{32,96},{64,0},{96,32},{1,65},{33,97},{65,1},{97,33},{2,66}... | collective-permute-start | bytes 776 | tf_op jit(solution)/shard_map/ppermute | solution.py:20
  317.1 3.1 fusion
  (248 shorter events, 135.1 us)
Async XLA Ops:
  7.2 69.1 %all-gather.4.cloned.1.call-start = ((), (), s32[]{:S(2)}) async-start(), calls=%async_computation.5 | async-start | bytes 9191424 | tf_op jit(solution)/shard_map/all_gather | solution.py:796
  28.3 14.9 %all-to-all-start = ((bf16[8,16,2048]{2,1,0:T(8,128)(2,1)}), bf16[8,16,2048]{2,1,0:T(8,128)(2,1)S(1)}, u32[]{:S(2)}, u32[]{:S(2)}) async-start(bf16[8,16,2048]{2,1,0:T(8,128)(2,1)} %bitcast.7), calls=%async_computation | async-start | bytes 1048576 | tf_op jit(solution)/shard_map/all_to_all | solution.py:820
  32.5 117.5 %all-gather.6.cloned.1.call-start = ((), (), s32[]{:S(2)}) async-start(), calls=%async_computation.6 | async-start | bytes 5242880 | tf_op jit(solution)/shard_map/all_gather | solution.py:830
  32.5 18.0 %collective-permute-start.7 = (bf16[2,512,256]{2,1,0:T(8,128)(2,1)}, bf16[2,512,256]{2,1,0:T(8,128)(2,1)}, u32[]{:S(2)}, u32[]{:S(2)}) collective-permute-start(bf16[2,512,256]{2,1,0:T(8,128)(2,1)} %w0), channel_id=1, source_target_pairs={{0,96},{32,0},{64,32},{96,64},{1,97},{33,1},{65,33},{97,65},{2,98}... | collective-permute-start | bytes 1572872 | tf_op jit(solution)/shard_map/ppermute | solution.py:20
  35.4 21.0 %collective-permute-start.8 = (bf16[2,512,256]{2,1,0:T(8,128)(2,1)}, bf16[2,512,256]{2,1,0:T(8,128)(2,1)}, u32[]{:S(2)}, u32[]{:S(2)}) collective-permute-start(bf16[2,512,256]{2,1,0:T(8,128)(2,1)} %w0), channel_id=1, source_target_pairs={{0,32},{32,64},{64,96},{96,0},{1,33},{33,65},{65,97},{97,1},{2,34}... | collective-permute-start | bytes 1572872 | tf_op jit(solution)/shard_map/ppermute | solution.py:20
  36.5 26.4 %collective-permute-start.5 = (bf16[4,128,512]{1,2,0:T(8,128)(2,1)S(1)}, bf16[4,128,512]{1,2,0:T(8,128)(2,1)}, u32[]{:S(2)}, u32[]{:S(2)}) collective-permute-start(bf16[4,128,512]{1,2,0:T(8,128)(2,1)S(1)} %pad_maximum_fusion.4), channel_id=1, source_target_pairs={{0,1},{1,2},{2,3},{3,0},{4,5},{5,6},{6,7},{7,4},{8,9},{9,10},{10,1... | collective-permute-start | bytes 1572872 | tf_op jit(solution)/shard_map/ppermute | solution.py:20
  38.1 26.2 %collective-permute-start.4 = (bf16[4,128,512]{1,2,0:T(8,128)(2,1)S(1)}, bf16[4,128,512]{1,2,0:T(8,128)(2,1)}, u32[]{:S(2)}, u32[]{:S(2)}) collective-permute-start(bf16[4,128,512]{1,2,0:T(8,128)(2,1)S(1)} %pad_maximum_fusion.4), channel_id=1, source_target_pairs={{0,2},{1,3},{2,0},{3,1},{4,6},{5,7},{6,4},{7,5},{8,10},{9,11},{10,... | collective-permute-start | bytes 1572872 | tf_op jit(solution)/shard_map/ppermute | solution.py:20
  41.0 24.5 %collective-permute-start.3 = (bf16[4,128,512]{1,2,0:T(8,128)(2,1)S(1)}, bf16[4,128,512]{1,2,0:T(8,128)(2,1)S(1)}, u32[]{:S(2)}, u32[]{:S(2)}) collective-permute-start(bf16[4,128,512]{1,2,0:T(8,128)(2,1)S(1)} %pad_maximum_fusion.4), channel_id=1, source_target_pairs={{0,3},{1,0},{2,1},{3,2},{4,7},{5,4},{6,5},{7,6},{8,11},{9,8},{10,9... | collective-permute-start | bytes 1572872 | tf_op jit(solution)/shard_map/ppermute | solution.py:20
  50.5 25.7 %all-to-all-start.1 = ((bf16[8,128,256]{2,1,0:T(8,128)(2,1)}), bf16[8,128,256]{2,1,0:T(8,128)(2,1)S(1)}, u32[]{:S(2)}, u32[]{:S(2)}) async-start(bf16[8,128,256]{2,1,0:T(8,128)(2,1)} %get-tuple-element.135), calls=%async_computation.1 | async-start | bytes 1048576 | tf_op jit(solution)/shard_map/all_to_all | solution.py:828
  55.1 239.6 %all-gather.8.cloned.1.call-start = ((), (), s32[]{:S(2)}) async-start(), calls=%async_computation.7 | async-start | bytes 1179648 | tf_op jit(solution)/shard_map/all_gather | solution.py:836
  56.4 14.5 %collective-permute-start.10 = (bf16[1,512,256]{2,1,0:T(8,128)(2,1)S(1)}, bf16[1,512,256]{2,1,0:T(8,128)(2,1)}, u32[]{:S(2)}, u32[]{:S(2)}) collective-permute-start(bf16[1,512,256]{2,1,0:T(8,128)(2,1)S(1)} %slice.122), channel_id=1, source_target_pairs={{0,96},{32,0},{64,32},{96,64},{1,97},{33,1},{65,33},{97,65},{2,98}... | collective-permute-start | bytes 786440 | tf_op jit(solution)/shard_map/ppermute | solution.py:20
  76.3 43.8 %collective-permute-start.17 = (bf16[4,512,512]{2,1,0:T(8,128)(2,1)}, bf16[4,512,512]{2,1,0:T(8,128)(2,1)}, u32[]{:S(2)}, u32[]{:S(2)}) collective-permute-start(bf16[4,512,512]{2,1,0:T(8,128)(2,1)} %pad_maximum_fusion.g_own), channel_id=1, source_target_pairs={{0,4},{4,0},{1,5},{5,1},{2,6},{6,2},{3,7},{7,3},{8,12},{12,8},{9,1... | collective-permute-start | bytes 6291464 | tf_op jit(solution)/shard_map/ppermute | solution.py:24
  84.9 20.7 %collective-permute-start.13 = (bf16[128,512]{1,0:T(8,128)(2,1)}, bf16[128,512]{1,0:T(8,128)(2,1)S(1)}, u32[]{:S(2)}, u32[]{:S(2)}) collective-permute-start(bf16[128,512]{1,0:T(8,128)(2,1)} %get-tuple-element.143), channel_id=1, source_target_pairs={{0,2},{1,3},{2,0},{3,1},{4,6},{5,7},{6,4},{7,5},{8,10},{9,11},{10,... | collective-permute-start | bytes 393224 | tf_op jit(solution)/shard_map/ppermute | solution.py:20
  120.1 14.4 %collective-permute-start.18 = (bf16[4,128,512]{2,1,0:T(8,128)(2,1)S(1)}, bf16[4,128,512]{2,1,0:T(8,128)(2,1)S(1)}, u32[]{:S(2)}, u32[]{:S(2)}) collective-permute-start(bf16[4,128,512]{2,1,0:T(8,128)(2,1)S(1)} %pad_maximum_fusion.6.resid), channel_id=1, source_target_pairs={{0,8},{8,16},{16,24},{24,0},{1,9},{9,17},{17,25},{25,1},{2,10},{10... | collective-permute-start | bytes 1572872 | tf_op jit(solution)/shard_map/ppermute | solution.py:20
  121.8 13.0 %collective-permute-start.19 = (bf16[4,128,512]{2,1,0:T(8,128)(2,1)S(1)}, bf16[4,128,512]{2,1,0:T(8,128)(2,1)}, u32[]{:S(2)}, u32[]{:S(2)}) collective-permute-start(bf16[4,128,512]{2,1,0:T(8,128)(2,1)S(1)} %pad_maximum_fusion.6.resid), channel_id=1, source_target_pairs={{0,24},{8,0},{16,8},{24,16},{1,25},{9,1},{17,9},{25,17},{2,26},{10... | collective-permute-start | bytes 1572872 | tf_op jit(solution)/shard_map/ppermute | solution.py:20
  183.8 133.3 %reduce-scatter.2.cloned.1.call-start = ((), (), s32[]{:S(2)}) async-start(), calls=%async_computation.8 | async-start | bytes 7864320 | tf_op jit(solution)/shard_map/reduce_scatter | solution.py:922
  183.9 17.1 %collective-permute-start.25 = (bf16[4,144,512]{2,1,0:T(8,128)(2,1)}, bf16[4,144,512]{2,1,0:T(8,128)(2,1)S(1)}, u32[]{:S(2)}, u32[]{:S(2)}) collective-permute-start(bf16[4,144,512]{2,1,0:T(8,128)(2,1)} %get-tuple-element.171), channel_id=1, source_target_pairs={{0,1},{1,2},{2,3},{3,0},{4,5},{5,6},{6,7},{7,4},{8,9},{9,10},{10,1... | collective-permute-start | bytes 1769480 | tf_op jit(solution)/shard_map/ppermute | solution.py:20
  185.2 29.8 %collective-permute-start.26 = (bf16[4,144,512]{2,1,0:T(8,128)(2,1)}, bf16[4,144,512]{2,1,0:T(8,128)(2,1)S(1)}, u32[]{:S(2)}, u32[]{:S(2)}) collective-permute-start(bf16[4,144,512]{2,1,0:T(8,128)(2,1)} %get-tuple-element.172), channel_id=1, source_target_pairs={{0,3},{1,0},{2,1},{3,2},{4,7},{5,4},{6,5},{7,6},{8,11},{9,8},{10,9... | collective-permute-start | bytes 1769480 | tf_op jit(solution)/shard_map/ppermute | solution.py:20
  187.2 27.9 %collective-permute-start.27 = (bf16[4,144,512]{2,1,0:T(8,128)(2,1)}, bf16[4,144,512]{2,1,0:T(8,128)(2,1)}, u32[]{:S(2)}, u32[]{:S(2)}) collective-permute-start(bf16[4,144,512]{2,1,0:T(8,128)(2,1)} %get-tuple-element.173), channel_id=1, source_target_pairs={{0,2},{1,3},{2,0},{3,1},{4,6},{5,7},{6,4},{7,5},{8,10},{9,11},{10,... | collective-permute-start | bytes 1769480 | tf_op jit(solution)/shard_map/ppermute | solution.py:20
  192.9 22.2 %collective-permute-start.29 = (bf16[128,2048]{1,0:T(8,128)(2,1)}, bf16[128,2048]{1,0:T(8,128)(2,1)}, u32[]{:S(2)}, u32[]{:S(2)}) collective-permute-start(bf16[128,2048]{1,0:T(8,128)(2,1)} %get-tuple-element.177), channel_id=1, source_target_pairs={{0,8},{8,16},{16,24},{24,0},{1,9},{9,17},{17,25},{25,1},{2,10},{10... | collective-permute-start | bytes 1572872 | tf_op jit(solution)/shard_map/ppermute | solution.py:20
  194.0 27.2 %collective-permute-start.30 = (bf16[128,2048]{1,0:T(8,128)(2,1)}, bf16[128,2048]{1,0:T(8,128)(2,1)}, u32[]{:S(2)}, u32[]{:S(2)}) collective-permute-start(bf16[128,2048]{1,0:T(8,128)(2,1)} %get-tuple-element.178), channel_id=1, source_target_pairs={{0,24},{8,0},{16,8},{24,16},{1,25},{9,1},{17,9},{25,17},{2,26},{10... | collective-permute-start | bytes 1572872 | tf_op jit(solution)/shard_map/ppermute | solution.py:20
  200.9 22.0 %collective-permute-start.31 = (bf16[128,2048]{1,0:T(8,128)(2,1)}, bf16[128,2048]{1,0:T(8,128)(2,1)}, u32[]{:S(2)}, u32[]{:S(2)}) collective-permute-start(bf16[128,2048]{1,0:T(8,128)(2,1)} %get-tuple-element.179), channel_id=1, source_target_pairs={{0,16},{8,24},{16,0},{24,8},{1,17},{9,25},{17,1},{25,9},{2,18},{10... | collective-permute-start | bytes 1572872 | tf_op jit(solution)/shard_map/ppermute | solution.py:20
  258.2 19.5 %collective-permute-start.42 = (bf16[128,1536]{1,0:T(8,128)(2,1)}, bf16[128,1536]{1,0:T(8,128)(2,1)S(1)}, u32[]{:S(2)}, u32[]{:S(2)}) collective-permute-start(bf16[128,1536]{1,0:T(8,128)(2,1)} %get-tuple-element.224.grad_proj), channel_id=1, source_target_pairs={{0,8},{8,16},{16,24},{24,0},{1,9},{9,17},{17,25},{25,1},{2,10},{10... | collective-permute-start | bytes 1179656 | tf_op jit(solution)/shard_map/ppermute | solution.py:20
  260.1 20.8 %collective-permute-start.41 = (bf16[128,1536]{1,0:T(8,128)(2,1)}, bf16[128,1536]{1,0:T(8,128)(2,1)S(1)}, u32[]{:S(2)}, u32[]{:S(2)}) collective-permute-start(bf16[128,1536]{1,0:T(8,128)(2,1)} %get-tuple-element.224.grad_proj), channel_id=1, source_target_pairs={{0,16},{8,24},{16,0},{24,8},{1,17},{9,25},{17,1},{25,9},{2,18},{10... | collective-permute-start | bytes 1179656 | tf_op jit(solution)/shard_map/ppermute | solution.py:20
  262.1 19.0 %collective-permute-start.40 = (bf16[128,1536]{1,0:T(8,128)(2,1)}, bf16[128,1536]{1,0:T(8,128)(2,1)}, u32[]{:S(2)}, u32[]{:S(2)}) collective-permute-start(bf16[128,1536]{1,0:T(8,128)(2,1)} %get-tuple-element.224.grad_proj), channel_id=1, source_target_pairs={{0,24},{8,0},{16,8},{24,16},{1,25},{9,1},{17,9},{25,17},{2,26},{10... | collective-permute-start | bytes 1179656 | tf_op jit(solution)/shard_map/ppermute | solution.py:20
  263.3 25.2 %collective-permute-start.47 = (bf16[128,512]{1,0:T(8,128)(2,1)}, bf16[128,512]{1,0:T(8,128)(2,1)}, u32[]{:S(2)}, u32[]{:S(2)}) collective-permute-start(bf16[128,512]{1,0:T(8,128)(2,1)} %get-tuple-element.234), channel_id=1, source_target_pairs={{0,2},{1,3},{2,0},{3,1},{4,6},{5,7},{6,4},{7,5},{8,10},{9,11},{10,... | collective-permute-start | bytes 393224 | tf_op jit(solution)/shard_map/ppermute | solution.py:20
  264.0 26.9 %all-to-all-start.2 = ((bf16[8,160,256]{2,1,0:T(8,128)(2,1)}), bf16[8,160,256]{2,1,0:T(8,128)(2,1)}, u32[]{:S(2)}, u32[]{:S(2)}) async-start(bf16[8,160,256]{2,1,0:T(8,128)(2,1)} %get-tuple-element.225), calls=%async_computation.2 | async-start | bytes 1310720 | tf_op jit(solution)/shard_map/all_to_all | solution.py:898
  290.9 14.1 %all-to-all-start.3 = ((bf16[8,32,1024]{2,1,0:T(8,128)(2,1)}), bf16[8,32,1024]{2,1,0:T(8,128)(2,1)S(1)}, u32[]{:S(2)}, u32[]{:S(2)}) async-start(bf16[8,32,1024]{2,1,0:T(8,128)(2,1)} %pad_maximum_fusion.7), calls=%async_computation.3 | async-start | bytes 1048576 | tf_op jit(solution)/shard_map/all_to_all | solution.py:929
  300.5 19.8 %collective-permute-start.44 = (bf16[64,2176]{1,0:T(8,128)(2,1)}, bf16[64,2176]{1,0:T(8,128)(2,1)S(1)}, u32[]{:S(2)}, u32[]{:S(2)}) collective-permute-start(bf16[64,2176]{1,0:T(8,128)(2,1)} %get-tuple-element.228), channel_id=1, source_target_pairs={{0,32},{32,64},{64,96},{96,0},{1,33},{33,65},{65,97},{97,1},{2,34}... | collective-permute-start | bytes 835592 | tf_op jit(solution)/shard_map/ppermute | solution.py:20
  300.9 19.3 %collective-permute-start.45 = (bf16[64,2176]{1,0:T(8,128)(2,1)}, bf16[64,2176]{1,0:T(8,128)(2,1)S(1)}, u32[]{:S(2)}, u32[]{:S(2)}) collective-permute-start(bf16[64,2176]{1,0:T(8,128)(2,1)} %get-tuple-element.229), channel_id=1, source_target_pairs={{0,96},{32,0},{64,32},{96,64},{1,97},{33,1},{65,33},{97,65},{2,98}... | collective-permute-start | bytes 835592 | tf_op jit(solution)/shard_map/ppermute | solution.py:20
  303.8 16.5 %collective-permute-start.46 = (bf16[64,2176]{1,0:T(8,128)(2,1)}, bf16[64,2176]{1,0:T(8,128)(2,1)S(1)}, u32[]{:S(2)}, u32[]{:S(2)}) collective-permute-start(bf16[64,2176]{1,0:T(8,128)(2,1)} %get-tuple-element.230), channel_id=1, source_target_pairs={{0,64},{32,96},{64,0},{96,32},{1,65},{33,97},{65,1},{97,33},{2,66}... | collective-permute-start | bytes 835592 | tf_op jit(solution)/shard_map/ppermute | solution.py:20
  305.8 14.4 %collective-permute-start.52 = (f32[1,64]{1,0:T(1,128)S(1)}, f32[1,64]{1,0:T(1,128)S(1)}, u32[]{:S(2)}, u32[]{:S(2)}) collective-permute-start(f32[1,64]{1,0:T(1,128)S(1)} %get-tuple-element.308), channel_id=1, source_target_pairs={{0,96},{32,0},{64,32},{96,64},{1,97},{33,1},{65,33},{97,65},{2,98}... | collective-permute-start | bytes 776 | tf_op jit(solution)/shard_map/ppermute | solution.py:20
  (62 other events, 507.9 us)
Sparse Core Ops, SparseCore 0:
  10.9 63.5 all-gather.3
  76.7 47.5 all-gather.5
  183.9 22.9 all-gather.7
  223.0 61.7 reduce-scatter.1
